TPU v7x, 512 devices: a whole 4x8x8 slice. The times are simulated.
512 devices in a mesh: space: 32 (over z_lo, y, core), mode: 16 (over z_hi, x).
Axes of the slice: x: 4, y: 8, z: 8 (z_hi: 4, z_lo: 2; z = z_hi * 2 + z_lo), core: 2. Of those that a mesh axis runs over, the one named last changes fastest.
Arguments:
- occupation_deviation: float32 [2048, 64, 4, 128], P('mode', 'space'), may hold values from -6 to 6
- initial_thermal_offset: float32 [64, 4, 128], P('space'), may hold values from -6 to 6
- branch_specific_warmth: float32 [2048], replicated, may hold values from 0.2 to 2
- courant_numbers: float32 [3, 2048], P(None, 'mode'), may hold values from 0.02 to 0.3
- sign_quadrant: int32 [2048], P('mode'), may hold values from 0 to 7
- scattering_matrix: bfloat16 [2048, 2048], P('mode'), may hold values from -1 to 1
Outputs:
- population_out: float32 [2048, 64, 4, 128], P('mode', 'space')
- thermal_offset: float32 [64, 4, 128], P('space')
All inputs are finite; a program needn't handle non-finite values.
Results may differ from a plain program's by a relative error of at most 0.002.
Values may be sent and summed in bfloat16 or wider, within the bound.
A program may use at most 64 MiB of HBM per device.

v0:
```python
import jax
import jax.numpy as jnp
from jax import lax
from jax.sharding import PartitionSpec as P

ITERS = 3


def padded_2(cells, sides, width):
    for axis, dim in sides:
        count = lax.axis_size(axis)
        head = lax.slice_in_dim(cells, 0, width, axis=dim)
        tail = lax.slice_in_dim(cells, cells.shape[dim] - width, cells.shape[dim], axis=dim)
        cells = jnp.concatenate(
            [
                lax.ppermute(tail, axis, [(i, (i + 1) % count) for i in range(count)]),
                cells,
                lax.ppermute(head, axis, [((i + 1) % count, i) for i in range(count)]),
            ],
            axis=dim,
        )
    return cells


def copy_for_each(x, axis):
    length = lax.axis_size(axis)
    return lax.all_to_all(jnp.broadcast_to(x[None], (length, *x.shape)), axis, 0, 0, tiled=True)


def joined_along(blocks, dim):
    shape = list(blocks.shape[1:])
    shape[dim] *= blocks.shape[0]
    return jnp.moveaxis(blocks, 0, dim).reshape(shape)


def gather_directly(x, axis, dim):
    blocks = copy_for_each(x, axis)
    return joined_along(blocks, dim)


def advect(lattice_wave_carry, courant_numbers, sign_quadrant):
    padded = padded_2(lattice_wave_carry, (("space", 1),), 1)
    advected = lattice_wave_carry
    for dim_index in range(3):
        if dim_index == 0:
            below_side = padded[:, :-2]
            above_side = padded[:, 2:]
        else:
            below_side = jnp.roll(lattice_wave_carry, 1, dim_index + 1)
            above_side = jnp.roll(lattice_wave_carry, -1, dim_index + 1)
        sign_bit = (sign_quadrant >> dim_index & 1).reshape(-1, 1, 1, 1)
        upwind = jnp.where(sign_bit == 1, above_side, below_side)
        advected = advected - courant_numbers[dim_index].reshape(-1, 1, 1, 1) * (
            lattice_wave_carry - upwind
        )
    return advected


def shards(
    occupation_deviation,
    initial_thermal_offset,
    branch_specific_warmth,
    courant_numbers,
    sign_quadrant,
    scattering_matrix,
):
    local_modes = occupation_deviation.shape[0]
    partition_extents = occupation_deviation.shape
    cell_count = partition_extents[1] * partition_extents[2] * partition_extents[3]
    first_mode = lax.axis_index("mode") * local_modes
    device_specific_warmth = lax.dynamic_slice_in_dim(
        branch_specific_warmth, first_mode, local_modes
    )
    summed_specific_warmth = jnp.sum(branch_specific_warmth)
    lattice_wave_carry = (
        occupation_deviation
        + device_specific_warmth.reshape(-1, 1, 1, 1) * initial_thermal_offset[None]
    )
    scattering_stripes = jnp.dot(
        scattering_matrix.astype(jnp.float32),
        branch_specific_warmth,
        precision=lax.Precision.HIGHEST,
    )
    full_matrix = lax.all_gather(scattering_matrix, "mode", axis=0, tiled=True)
    thermal_offset = jnp.zeros(partition_extents[1:], jnp.float32)
    for iteration in range(ITERS):
        upstream_occupation = advect(lattice_wave_carry, courant_numbers, sign_quadrant)
        moved_bf = upstream_occupation.astype(jnp.bfloat16)
        local_flat_bf = moved_bf.reshape(local_modes, cell_count)
        all_modes = lax.all_to_all(local_flat_bf, "mode", split_axis=1, concat_axis=0, tiled=True)
        block_product = jnp.dot(full_matrix, all_modes, preferred_element_type=jnp.float32)
        block_energy = jnp.dot(
            branch_specific_warmth, all_modes.astype(jnp.float32), precision=lax.Precision.HIGHEST
        )
        scattering_applied = lax.all_to_all(
            block_product, "mode", split_axis=0, concat_axis=1, tiled=True
        )
        internal_warmth_field = gather_directly(block_energy, "mode", 0)
        thermal_offset = (internal_warmth_field / summed_specific_warmth).reshape(
            partition_extents[1:]
        )
        lattice_wave_carry = (
            upstream_occupation
            - scattering_applied.reshape(partition_extents)
            + scattering_stripes.reshape(-1, 1, 1, 1) * thermal_offset[None]
        )
    return (lattice_wave_carry, thermal_offset)


def solution(mesh):
    placed = (
        P("mode", "space", None, None),
        P("space", None, None),
        P(),
        P(None, "mode"),
        P("mode"),
        P("mode", None),
    )
    return jax.shard_map(
        shards,
        mesh=mesh,
        in_specs=placed,
        out_specs=(P("mode", "space", None, None), P("space", None, None)),
        check_vma=False,
    )
```

profile of v0, /device:TPU:16, one launch (start us, length us, event | category | flops | bytes accessed | tf_op | source)
XLA Modules:
  0.0 312.7 jit_solution(900750973917751772)
XLA Ops:
  12.8 2.4 collective-permute-start.1
  16.9 3.6 %collective-permute-done.1 = f32[128,1,4,128]{0,3,2,1:T(8,128)S(1)} collective-permute-done((f32[128,1,4,128]{0,3,2,1:T(8,128)S(1)}, f32[128,1,4,128]{0,3,2,1:T(8,128)S(1)}, u32[]{:S(2)}, u32[]{:S(2)}) %collective-permute-start.1) | collective-permute-done | bytes 262176 | tf_op jit(solution)/shard_map/ppermute | solution.py:16
  20.8 30.4 %all_to_all.123 = bf16[128,16,64]{0,2,1:T(8,128)(2,1)S(1)} all-to-all(bf16[128,16,64]{0,2,1:T(8,128)(2,1)S(1)} %bitcast.99), channel_id=1, replica_groups=mesh['space'=32,'mode'=16] {'mode'}, dimensions={1} | all-to-all | bytes 524288 | tf_op jit(solution)/shard_map/all_to_all | solution.py:90
  52.1 6.0 %all-to-all-start.2 = ((f32[16,1,64]{2,1,0:T(1,128)}), f32[16,1,64]{2,1,0:T(1,128)S(1)}, u32[]{:S(2)}, u32[]{:S(2)}) async-start(f32[16,1,64]{2,1,0:T(1,128)} %broadcast_in_dim.58), calls=%async_computation.2 | async-start | bytes 16384 | tf_op jit(solution)/shard_map/all_to_all | solution.py:27
  58.1 86.2 %all-gather.2.cloned.1.call-done = bf16[2048,2048]{1,0:T(8,128)(2,1)} async-done(((bf16[128,2048]{1,0:T(8,128)(2,1)}), bf16[2048,2048]{1,0:T(8,128)(2,1)}) %all-gather.2.cloned.1.call-update) | async-done | bytes 8388624 | tf_op jit(solution)/shard_map/all_gather | solution.py:84
  144.3 6.0 %convolution_bitcast_fusion.2 = f32[8,16,8,128]{3,2,1,0:T(8,128)S(1)} fusion(bf16[2048,2048]{1,0:T(8,128)(2,1)} %all-gather.2.cloned.1.call-done, bf16[128,16,64]{0,2,1:T(8,128)(2,1)S(1)} %all_to_all.123), kind=kOutput, calls=%fused_computation.2 | convolution fusion | flops 536870912 | bytes 9175040 | tf_op jit(solution)/shard_map/dot_general | solution.py:91
  151.2 6.2 %all-to-all-start.1 = ((f32[16,128,64]{1,2,0:T(8,128)}), f32[16,128,64]{1,2,0:T(8,128)S(1)}, u32[]{:S(2)}, u32[]{:S(2)}) async-start(f32[16,128,64]{1,2,0:T(8,128)} %bitcast.94), calls=%async_computation.1 | async-start | bytes 1048576 | tf_op jit(solution)/shard_map/all_to_all | solution.py:95
  159.3 15.9 %all-to-all-done.1 = f32[16,128,64]{1,2,0:T(8,128)S(1)} async-done(((f32[16,128,64]{1,2,0:T(8,128)}), f32[16,128,64]{1,2,0:T(8,128)S(1)}, u32[]{:S(2)}, u32[]{:S(2)}) %all-to-all-start.1) | async-done | bytes 524320 | tf_op jit(solution)/shard_map/all_to_all | solution.py:95
  177.5 2.4 collective-permute-start.3
  181.3 3.8 %collective-permute-done.3 = f32[128,1,4,128]{0,3,2,1:T(8,128)S(1)} collective-permute-done((f32[128,1,4,128]{0,3,2,1:T(8,128)S(1)}, f32[128,1,4,128]{0,3,2,1:T(8,128)S(1)}, u32[]{:S(2)}, u32[]{:S(2)}) %collective-permute-start.3) | collective-permute-done | bytes 262176 | tf_op jit(solution)/shard_map/ppermute | solution.py:16
  185.5 16.2 %all_to_all.124 = bf16[128,16,64]{0,2,1:T(8,128)(2,1)S(1)} all-to-all(bf16[128,16,64]{0,2,1:T(8,128)(2,1)S(1)} %bitcast.100), channel_id=1, replica_groups=mesh['space'=32,'mode'=16] {'mode'}, dimensions={1} | all-to-all | bytes 524288 | tf_op jit(solution)/shard_map/all_to_all | solution.py:90
  202.6 3.8 %all-to-all-start.5 = ((f32[16,1,64]{2,1,0:T(1,128)}), f32[16,1,64]{2,1,0:T(1,128)S(1)}, u32[]{:S(2)}, u32[]{:S(2)}) async-start(f32[16,1,64]{2,1,0:T(1,128)} %broadcast_in_dim.59), calls=%async_computation.5 | async-start | bytes 16384 | tf_op jit(solution)/shard_map/all_to_all | solution.py:27
  206.4 6.0 %convolution_bitcast_fusion.1 = f32[8,16,8,128]{3,2,1,0:T(8,128)S(1)} fusion(bf16[2048,2048]{1,0:T(8,128)(2,1)} %all-gather.2.cloned.1.call-done, bf16[128,16,64]{0,2,1:T(8,128)(2,1)S(1)} %all_to_all.124), kind=kOutput, calls=%fused_computation.1 | convolution fusion | flops 536870912 | bytes 9175040 | tf_op jit(solution)/shard_map/dot_general | solution.py:91
  213.3 2.9 all-to-all-done.5
  216.2 6.7 %all-to-all-start.4 = ((f32[16,128,64]{1,2,0:T(8,128)}), f32[16,128,64]{1,2,0:T(8,128)S(1)}, u32[]{:S(2)}, u32[]{:S(2)}) async-start(f32[16,128,64]{1,2,0:T(8,128)} %bitcast.93), calls=%async_computation.4 | async-start | bytes 1048576 | tf_op jit(solution)/shard_map/all_to_all | solution.py:95
  223.6 14.6 %all-to-all-done.4 = f32[16,128,64]{1,2,0:T(8,128)S(1)} async-done(((f32[16,128,64]{1,2,0:T(8,128)}), f32[16,128,64]{1,2,0:T(8,128)S(1)}, u32[]{:S(2)}, u32[]{:S(2)}) %all-to-all-start.4) | async-done | bytes 524320 | tf_op jit(solution)/shard_map/all_to_all | solution.py:95
  240.6 2.4 collective-permute-start.5
  244.5 3.8 %collective-permute-done.5 = f32[128,1,4,128]{0,3,2,1:T(8,128)S(1)} collective-permute-done((f32[128,1,4,128]{0,3,2,1:T(8,128)S(1)}, f32[128,1,4,128]{0,3,2,1:T(8,128)S(1)}, u32[]{:S(2)}, u32[]{:S(2)}) %collective-permute-start.5) | collective-permute-done | bytes 262176 | tf_op jit(solution)/shard_map/ppermute | solution.py:16
  248.6 17.0 %all_to_all.125 = bf16[128,16,64]{0,2,1:T(8,128)(2,1)S(1)} all-to-all(bf16[128,16,64]{0,2,1:T(8,128)(2,1)S(1)} %bitcast.98), channel_id=1, replica_groups=mesh['space'=32,'mode'=16] {'mode'}, dimensions={1} | all-to-all | bytes 524288 | tf_op jit(solution)/shard_map/all_to_all | solution.py:90
  266.5 4.6 %all-to-all-start.8 = ((f32[16,1,64]{2,1,0:T(1,128)}), f32[16,1,64]{2,1,0:T(1,128)S(1)}, u32[]{:S(2)}, u32[]{:S(2)}) async-start(f32[16,1,64]{2,1,0:T(1,128)} %broadcast_in_dim.60), calls=%async_computation.8 | async-start | bytes 16384 | tf_op jit(solution)/shard_map/all_to_all | solution.py:27
  271.2 6.0 %convolution_bitcast_fusion = f32[8,16,8,128]{3,2,1,0:T(8,128)S(1)} fusion(bf16[2048,2048]{1,0:T(8,128)(2,1)} %all-gather.2.cloned.1.call-done, bf16[128,16,64]{0,2,1:T(8,128)(2,1)S(1)} %all_to_all.125), kind=kOutput, calls=%fused_computation | convolution fusion | flops 536870912 | bytes 9175040 | tf_op jit(solution)/shard_map/dot_general | solution.py:91
  278.1 2.9 all-to-all-done.8
  281.0 6.7 %all-to-all-start.7 = ((f32[16,128,64]{1,2,0:T(8,128)}), f32[16,128,64]{1,2,0:T(8,128)S(1)}, u32[]{:S(2)}, u32[]{:S(2)}) async-start(f32[16,128,64]{1,2,0:T(8,128)} %bitcast.92), calls=%async_computation.7 | async-start | bytes 1048576 | tf_op jit(solution)/shard_map/all_to_all | solution.py:95
  288.5 16.2 %all-to-all-done.7 = f32[16,128,64]{1,2,0:T(8,128)S(1)} async-done(((f32[16,128,64]{1,2,0:T(8,128)}), f32[16,128,64]{1,2,0:T(8,128)S(1)}, u32[]{:S(2)}, u32[]{:S(2)}) %all-to-all-start.7) | async-done | bytes 524320 | tf_op jit(solution)/shard_map/all_to_all | solution.py:95
  (59 shorter events, 25.6 us)
Async XLA Ops:
  7.2 44.0 %copy-start.1 = (f32[2048]{0:T(1024)S(1)}, f32[2048]{0:T(1024)}, u32[]{:S(2)}) copy-start(f32[2048]{0:T(1024)} %param.8) | copy-start | bytes 24580
  7.2 137.1 %all-gather.2.cloned.1.call-start = ((), (), s32[]{:S(2)}) async-start(), calls=%async_computation.9 | async-start | bytes 8912896 | tf_op jit(solution)/shard_map/all_gather | solution.py:84
  10.9 6.0 %collective-permute-start = (f32[128,1,4,128]{0,3,2,1:T(8,128)S(1)}, f32[128,1,4,128]{0,3,2,1:T(8,128)S(1)}, u32[]{:S(2)}, u32[]{:S(2)}) collective-permute-start(f32[128,1,4,128]{0,3,2,1:T(8,128)S(1)} %get-tuple-element.32), channel_id=1, source_target_pairs={{16,0},{32,16},{48,32},{64,48},{80,64},{96,80},{112,96},{128,112},... | collective-permute-start | bytes 786440 | tf_op jit(solution)/shard_map/ppermute | solution.py:18
  12.8 7.7 %collective-permute-start.1 = (f32[128,1,4,128]{0,3,2,1:T(8,128)S(1)}, f32[128,1,4,128]{0,3,2,1:T(8,128)S(1)}, u32[]{:S(2)}, u32[]{:S(2)}) collective-permute-start(f32[128,1,4,128]{0,3,2,1:T(8,128)S(1)} %get-tuple-element.33), channel_id=1, source_target_pairs={{0,16},{16,32},{32,48},{48,64},{64,80},{80,96},{96,112},{112,128},... | collective-permute-start | bytes 786440 | tf_op jit(solution)/shard_map/ppermute | solution.py:16
  16.9 141.1 %copy-start = (bf16[128,2048]{1,0:T(8,128)(2,1)S(1)}, bf16[128,2048]{1,0:T(8,128)(2,1)}, u32[]{:S(2)}) copy-start(bf16[128,2048]{1,0:T(8,128)(2,1)} %param.11) | copy-start | bytes 1572868
  52.1 99.1 %all-to-all-start.2 = ((f32[16,1,64]{2,1,0:T(1,128)}), f32[16,1,64]{2,1,0:T(1,128)S(1)}, u32[]{:S(2)}, u32[]{:S(2)}) async-start(f32[16,1,64]{2,1,0:T(1,128)} %broadcast_in_dim.58), calls=%async_computation.2 | async-start | bytes 16384 | tf_op jit(solution)/shard_map/all_to_all | solution.py:27
  151.2 23.9 %all-to-all-start.1 = ((f32[16,128,64]{1,2,0:T(8,128)}), f32[16,128,64]{1,2,0:T(8,128)S(1)}, u32[]{:S(2)}, u32[]{:S(2)}) async-start(f32[16,128,64]{1,2,0:T(8,128)} %bitcast.94), calls=%async_computation.1 | async-start | bytes 1048576 | tf_op jit(solution)/shard_map/all_to_all | solution.py:95
  175.5 5.8 %collective-permute-start.2 = (f32[128,1,4,128]{0,3,2,1:T(8,128)S(1)}, f32[128,1,4,128]{0,3,2,1:T(8,128)S(1)}, u32[]{:S(2)}, u32[]{:S(2)}) collective-permute-start(f32[128,1,4,128]{0,3,2,1:T(8,128)S(1)} %get-tuple-element.22), channel_id=1, source_target_pairs={{16,0},{32,16},{48,32},{64,48},{80,64},{96,80},{112,96},{128,112},... | collective-permute-start | bytes 786440 | tf_op jit(solution)/shard_map/ppermute | solution.py:18
  177.5 7.7 %collective-permute-start.3 = (f32[128,1,4,128]{0,3,2,1:T(8,128)S(1)}, f32[128,1,4,128]{0,3,2,1:T(8,128)S(1)}, u32[]{:S(2)}, u32[]{:S(2)}) collective-permute-start(f32[128,1,4,128]{0,3,2,1:T(8,128)S(1)} %get-tuple-element.23), channel_id=1, source_target_pairs={{0,16},{16,32},{32,48},{48,64},{64,80},{80,96},{96,112},{112,128},... | collective-permute-start | bytes 786440 | tf_op jit(solution)/shard_map/ppermute | solution.py:16
  202.6 13.6 %all-to-all-start.5 = ((f32[16,1,64]{2,1,0:T(1,128)}), f32[16,1,64]{2,1,0:T(1,128)S(1)}, u32[]{:S(2)}, u32[]{:S(2)}) async-start(f32[16,1,64]{2,1,0:T(1,128)} %broadcast_in_dim.59), calls=%async_computation.5 | async-start | bytes 16384 | tf_op jit(solution)/shard_map/all_to_all | solution.py:27
  216.2 22.1 %all-to-all-start.4 = ((f32[16,128,64]{1,2,0:T(8,128)}), f32[16,128,64]{1,2,0:T(8,128)S(1)}, u32[]{:S(2)}, u32[]{:S(2)}) async-start(f32[16,128,64]{1,2,0:T(8,128)} %bitcast.93), calls=%async_computation.4 | async-start | bytes 1048576 | tf_op jit(solution)/shard_map/all_to_all | solution.py:95
  238.7 5.8 %collective-permute-start.4 = (f32[128,1,4,128]{0,3,2,1:T(8,128)S(1)}, f32[128,1,4,128]{0,3,2,1:T(8,128)S(1)}, u32[]{:S(2)}, u32[]{:S(2)}) collective-permute-start(f32[128,1,4,128]{0,3,2,1:T(8,128)S(1)} %get-tuple-element.12), channel_id=1, source_target_pairs={{16,0},{32,16},{48,32},{64,48},{80,64},{96,80},{112,96},{128,112},... | collective-permute-start | bytes 786440 | tf_op jit(solution)/shard_map/ppermute | solution.py:18
  240.6 7.7 %collective-permute-start.5 = (f32[128,1,4,128]{0,3,2,1:T(8,128)S(1)}, f32[128,1,4,128]{0,3,2,1:T(8,128)S(1)}, u32[]{:S(2)}, u32[]{:S(2)}) collective-permute-start(f32[128,1,4,128]{0,3,2,1:T(8,128)S(1)} %get-tuple-element.13), channel_id=1, source_target_pairs={{0,16},{16,32},{32,48},{48,64},{64,80},{80,96},{96,112},{112,128},... | collective-permute-start | bytes 786440 | tf_op jit(solution)/shard_map/ppermute | solution.py:16
  266.5 14.5 %all-to-all-start.8 = ((f32[16,1,64]{2,1,0:T(1,128)}), f32[16,1,64]{2,1,0:T(1,128)S(1)}, u32[]{:S(2)}, u32[]{:S(2)}) async-start(f32[16,1,64]{2,1,0:T(1,128)} %broadcast_in_dim.60), calls=%async_computation.8 | async-start | bytes 16384 | tf_op jit(solution)/shard_map/all_to_all | solution.py:27
  281.0 23.6 %all-to-all-start.7 = ((f32[16,128,64]{1,2,0:T(8,128)}), f32[16,128,64]{1,2,0:T(8,128)S(1)}, u32[]{:S(2)}, u32[]{:S(2)}) async-start(f32[16,128,64]{1,2,0:T(8,128)} %bitcast.92), calls=%async_computation.7 | async-start | bytes 1048576 | tf_op jit(solution)/shard_map/all_to_all | solution.py:95
  288.5 17.4 %copy-start.2 = (f32[2,4,128]{2,1,0:T(4,128)}, f32[2,4,128]{2,1,0:T(4,128)S(1)}, u32[]{:S(2)}) copy-start(f32[2,4,128]{2,1,0:T(4,128)S(1)} %div.42) | copy-start | bytes 12292
Sparse Core Ops, SparseCore 0:
  11.0 133.2 all-gather.1
where the time goes:
time: 314 us; the launch traced here: 313 us
  waiting for transfers between devices  153 us (49%)
  blocking collectives  63.5 us (20%)
  starting transfers between devices  47 us (15%)
  matrix products  19.5 us (6%)
  between operations  14.3 us (5%)
  local copies, waits for them, and re-layouts  9.09 us (3%)
  other arithmetic  5.87 us (2%)
    all_gather x1, waiting for transfers between devices, shards(): full_matrix = lax.all_gather(scattering_matrix, 'mode', axis=0, tiled=True)  86.2 us
    all_to_all x3, blocking collectives, shards(): lax.all_to_all(local_flat_bf, 'mode', split_axis=1, concat_axis=0, tiled=...  63.5 us
    all_to_all x3, waiting for transfers between devices, shards(): lax.all_to_all(block_product, 'mode', split_axis=0, concat_axis=1, tiled=...  46.7 us
    all_to_all x3, starting transfers between devices, shards(): lax.all_to_all(block_product, 'mode', split_axis=0, concat_axis=1, tiled=...  19.6 us
    dot_general x3, matrix products, shards(): jnp.dot(full_matrix, all_modes, preferred_element_type=jnp.float32)  18.1 us
    all_to_all x3, starting transfers between devices, copy_for_each(): lax.all_to_all(jnp.broadcast_to(x[None], (length, *x.shape)), axis, 0, 0,...  14.4 us
    ppermute x3, waiting for transfers between devices, padded_2(): lax.ppermute(tail, axis, [(i, (i + 1) % count) for i in range(count)])  11.2 us
    ppermute x3, starting transfers between devices, padded_2(): lax.ppermute(tail, axis, [(i, (i + 1) % count) for i in range(count)])  7.22 us
  transfers between devices with their start and end apart: 13, of which 11 were waited for; matrix products, arithmetic and copies ran while one was open for 10% of the time, Pallas kernels for 0%

commit v1 on v0

v1 whole, which is shorter than its diff:
```python
import functools

import jax
import jax.numpy as jnp
from jax import lax
from jax.experimental import pallas as pl
from jax.experimental.pallas import tpu as pltpu
from jax.sharding import PartitionSpec as P

ITERS = 3
NA, NB = 4, 4
NK = NA * NB
NS = 32
MODES = 128
M = NK * MODES
MESH = pl.DeviceIdType.MESH

SLOTS = [
    ("p", 0), ("r", 0, 0), ("p", 1), ("r", 0, 1), ("p", 2), ("r", 0, 2), ("r", 1, 0), ("r", 0, 3),
    ("r", 1, 1), ("r", 1, 2), ("r", 2, 0), ("r", 1, 3), ("r", 2, 1), ("r", 2, 2), ("r", 2, 3),
]
SEQ = {item: n for n, item in enumerate(SLOTS)}


def kernel(
    occ_ref, t0_ref, warm_ref, cour_ref, sign_ref, s_ref,
    out_ref, therm_ref,
    full, sent, state, final, landed, lhs, wlhs, relax, xs, xr, zs, zr, moved,
    own_sem, g_send, g_recv, c_send, c_recv, in_send, in_recv, x_send, x_recv, z_send, z_recv, o_send, o_recv,
):
    s = lax.axis_index("space")
    k = lax.axis_index("mode")
    a, b = k // NB, k % NB
    lo = s // 16
    core = s % 2

    def dev(space, mode):
        return {"space": space, "mode": mode}

    def wrap(v, n):
        return lax.rem(v + 4 * n, n)

    def x_peer(sg):
        return dev(s, a * NB + wrap(b + sg, NB))

    def z_peer(sg):
        crosses = lo if sg > 0 else 1 - lo
        return dev(lax.rem(s + 16, NS), wrap(a + sg * crosses, NA) * NB + b)

    partner = dev(s + 1 - 2 * core, k)
    right, left = dev(wrap(s + 1, NS), k), dev(wrap(s - 1, NS), k)
    z_next, z_prev = dev(s, wrap(k + 1, NK)), dev(s, wrap(k - 1, NK))

    def mode_peer(d):
        return wrap(k + d, NK)

    own = pltpu.make_async_copy(s_ref, full.at[a, b], own_sem)
    own.start()
    barrier = pltpu.get_barrier_semaphore()

    @pl.loop(1, NK)
    def _(d):
        pl.semaphore_signal(barrier, inc=1, device_id=dev(s, mode_peer(d)), device_id_type=MESH)

    for peer in (right, left, z_peer(1), z_peer(-1)):
        pl.semaphore_signal(barrier, inc=1, device_id=peer, device_id_type=MESH)

    warm_col = jnp.transpose(jnp.broadcast_to(warm_ref[pl.ds(k, 1), :], (MODES, MODES)))
    for xy in range(8):
        cells = occ_ref[pl.ds(xy, MODES, stride=8), :] + warm_col * t0_ref[xy:xy + 1, :]
        sent[:, pl.ds(xy * 8, 8), :] = jnp.transpose(cells).reshape(NK, 8, MODES)
    sign = sign_ref[...]
    row = lax.broadcasted_iota(jnp.int32, (8, MODES), 0)
    coef = jnp.zeros((8, MODES), jnp.float32)
    for d in range(3):
        bit = jnp.broadcast_to((sign >> d) & 1, (8, MODES))
        c = jnp.broadcast_to(cour_ref[d:d + 1, :], (8, MODES))
        coef = jnp.where(row == 2 * d, jnp.where(bit == 0, c, 0.0), coef)
        coef = jnp.where(row == 2 * d + 1, jnp.where(bit == 1, c, 0.0), coef)
    sent[:, 64:72, :] = jnp.broadcast_to(coef[None], (NK, 8, MODES))

    pl.semaphore_wait(barrier, NK - 1 + 4)

    def a2a(src, dst, send, recv, d):
        there = mode_peer(d)
        return pltpu.make_async_remote_copy(
            src_ref=src.at[there], dst_ref=dst.at[k], send_sem=send.at[d], recv_sem=recv.at[d],
            device_id=dev(s, there), device_id_type=MESH,
        )

    @pl.loop(1, NK)
    def _(d):
        a2a(sent, state, in_send, in_recv, d).start()

    state[k] = sent[k]

    own.wait()

    def piece(link, sg, item):
        color = (0 if sg > 0 else 1) if (link == "x") == (item[0] == "r") else (2 if sg > 0 else 3)
        return color

    def z_from(sg, i):
        follows = (1 - lo) if sg > 0 else lo
        return wrap(a - sg * (i + follows), NA)

    def x_from(sg, i):
        return wrap(b - sg * i, NB)

    def gcopy(link, sg, item):
        li = (0 if link == "x" else 2) + (0 if sg > 0 else 1)
        n = SEQ[item]
        color = piece(link, sg, item)
        i = item[1]
        if link == "x":
            row_ = a if item[0] == "p" else wrap(a - sg * item[2], NA)
            at = (row_, x_from(sg, i))
            peer = x_peer(sg)
        else:
            col_ = b if item[0] == "p" else wrap(b - sg * item[2], NB)
            at = (z_from(sg, i), col_)
            peer = z_peer(sg)
        block = full.at[at[0], at[1], core * 4 + color]
        return pltpu.make_async_remote_copy(
            src_ref=block, dst_ref=block, send_sem=g_send.at[li, n], recv_sem=g_recv.at[li, n],
            device_id=peer, device_id_type=MESH,
        )

    waited = set()

    def wait_recv(link, sg, item):
        if (link, sg, item) not in waited:
            waited.add((link, sg, item))
            gcopy(link, sg, item).wait_recv()

    def leads(sg):
        return lo == (1 if sg > 0 else 0)

    core_copies = []

    def core_copy(color, n, block):
        copy = pltpu.make_async_remote_copy(
            src_ref=block, dst_ref=block, send_sem=c_send.at[color, n], recv_sem=c_recv.at[color, n],
            device_id=partner, device_id_type=MESH,
        )
        copy.start()
        core_copies.append(copy)

    def issue(link, sg, item):
        other = "z" if link == "x" else "x"
        i = item[1]
        if item[0] == "r" and item[2] > 0:
            wait_recv(other, sg, ("p", item[2] - 1))
        before = (item[0], i - 1, *item[2:]) if i > 0 else None
        if link == "x":
            if before:
                wait_recv(link, sg, before)
            gcopy(link, sg, item).start()
        else:
            if before:
                wait_recv(link, sg, before)
            first = leads(sg)

            @pl.when(first)
            def _():
                gcopy(link, sg, item).start()

            @pl.when(jnp.logical_not(first))
            def _():
                gcopy(link, sg, item).wait_recv()
                gcopy(link, sg, item).start()

    def wait_recv(link, sg, item):
        if (link, sg, item) in waited:
            return
        waited.add((link, sg, item))
        if link == "x":
            gcopy(link, sg, item).wait_recv()
        else:
            @pl.when(leads(sg))
            def _():
                gcopy(link, sg, item).wait_recv()

    for item in SLOTS:
        for link in ("x", "z"):
            for sg in (1, -1):
                issue(link, sg, item)
        if item == ("r", 0, 3):
            pass

    for link in ("x", "z"):
        for sg in (1, -1):
            for item in SLOTS:
                wait_recv(link, sg, item)
    for sg in (1, -1):
        cx, cz = (0, 2) if sg > 0 else (1, 3)
        for q in range(1, 4):
            core_copy(cx, q - 1, full.at[wrap(a - sg * q, NA), b, core * 4 + cx])
            core_copy(cz, q - 1, full.at[a, wrap(b - sg * q, NB), core * 4 + cz])
        for i in range(3):
            core_copy(cx, 3 + i, full.at[:, wrap(b - sg * (i + 1), NB), core * 4 + cx])
            core_copy(cz, 3 + i, full.at[wrap(a - sg * (i + 1), NA), :, core * 4 + cz])

    @pl.loop(1, NK)
    def _(d):
        a2a(sent, state, in_send, in_recv, d).wait_recv()

    total = jnp.sum(warm_ref[...])
    row16 = lax.broadcasted_iota(jnp.int32, (16, MODES), 0)
    for j in range(NK):
        w = jnp.broadcast_to(warm_ref[j:j + 1, :], (16, MODES))
        hi = w.astype(jnp.bfloat16).astype(jnp.float32)
        mid = (w - hi).astype(jnp.bfloat16).astype(jnp.float32)
        low = w - hi - mid
        parts = jnp.where(row16 == 0, hi, jnp.where(row16 == 1, mid, jnp.where(row16 == 2, low, 0.0)))
        wlhs[:, j * MODES:(j + 1) * MODES] = parts.astype(jnp.bfloat16)

    zi = lax.broadcasted_iota(jnp.int32, (8, 8, MODES), 1)

    def xcopy(t, way):
        return pltpu.make_async_remote_copy(
            src_ref=xs.at[t, way], dst_ref=xr.at[t, way], send_sem=x_send.at[t, way], recv_sem=x_recv.at[t, way],
            device_id=right if way == 0 else left, device_id_type=MESH,
        )

    def zcopy(t, way):
        return pltpu.make_async_remote_copy(
            src_ref=zs.at[t, way], dst_ref=zr.at[t, way], send_sem=z_send.at[t, way], recv_sem=z_recv.at[t, way],
            device_id=z_next if way == 0 else z_prev, device_id_type=MESH,
        )

    for t in range(ITERS):
        xs[t, 0] = state[:, 32:64, :].astype(jnp.bfloat16)
        xcopy(t, 0).start()
        xs[t, 1] = state[:, 0:32, :].astype(jnp.bfloat16)
        xcopy(t, 1).start()
        for j in range(NK):
            zs[t, 0, j] = state[j, pl.ds(7, 8, stride=8), :]
            zs[t, 1, j] = state[j, pl.ds(0, 8, stride=8), :]
        zcopy(t, 0).start()
        zcopy(t, 1).start()
        for way in range(2):
            xcopy(t, way).wait_recv()
            zcopy(t, way).wait_recv()

        def advect(j, energy):
            st = state[j, 0:64, :].reshape(8, 8, MODES)
            cf = [state[j, pl.ds(64 + r, 1), :].reshape(1, 1, MODES) for r in range(6)]
            below = xr[t, 0, j].astype(jnp.float32).reshape(4, 8, MODES)
            above = xr[t, 1, j].astype(jnp.float32).reshape(4, 8, MODES)
            x_below = jnp.concatenate([below, st[0:4]], axis=0)
            x_above = jnp.concatenate([st[4:8], above], axis=0)
            y_below = jnp.concatenate([st[3:4], st[0:3], st[7:8], st[4:7]], axis=0)
            y_above = jnp.concatenate([st[1:4], st[0:1], st[5:8], st[4:5]], axis=0)
            z_lower = zr[t, 0, j].reshape(8, 1, MODES)
            z_upper = zr[t, 1, j].reshape(8, 1, MODES)
            z_below = jnp.where(zi == 0, z_lower, jnp.roll(st, 1, 1))
            z_above = jnp.where(zi == 7, z_upper, jnp.roll(st, -1, 1))
            mv = st
            for d, (lower, upper) in enumerate(((x_below, x_above), (y_below, y_above), (z_below, z_above))):
                mv = mv - (cf[2 * d] * (st - lower) + cf[2 * d + 1] * (st - upper))
            mv = mv.reshape(64, MODES)
            mv_bf = mv.astype(jnp.bfloat16)
            moved[j] = mv
            lhs[:, pl.ds(pl.multiple_of(j * MODES, MODES), MODES)] = mv_bf
            return energy + mv_bf.astype(jnp.float32) * warm_ref[pl.ds(j, 1), :]

        energy = lax.fori_loop(0, NK, advect, jnp.zeros((64, MODES), jnp.float32))
        thermal = jnp.sum(energy, axis=1, keepdims=True) / total
        thermal = jnp.broadcast_to(thermal, (64, MODES))

        if t == 0:
            for copy in core_copies:
                copy.wait_recv()

        nt = (((1,), (1,)), ((), ()))
        target = final if t == ITERS - 1 else state

        @pl.loop(0, NK // 2)
        def _(n):
            w = full[n // 2, pl.ds((n % 2) * 2, 2)].reshape(2 * MODES, M)
            product = lax.dot_general(lhs[...], w, nt, preferred_element_type=jnp.float32)
            if t == 0:
                parts = lax.dot_general(wlhs[...], w, nt, preferred_element_type=jnp.float32)
                both = parts[0:1] + parts[1:2] + parts[2:3]
                relax[2 * n] = jnp.broadcast_to(both[:, :MODES], (8, MODES))
                relax[2 * n + 1] = jnp.broadcast_to(both[:, MODES:], (8, MODES))
            for h in range(2):
                j = 2 * n + h
                pr = product[:, h * MODES:(h + 1) * MODES]
                target[j, 0:64, :] = moved[j] - pr + relax[j, 0:1] * thermal

    lane = lax.broadcasted_iota(jnp.int32, (8, 8, MODES), 2)
    mine = jnp.sum(jnp.where(lane == 8 * k + zi, thermal.reshape(8, 8, MODES), 0.0), axis=1)
    final[:, 64:72, :] = jnp.broadcast_to(mine[None], (NK, 8, MODES))

    @pl.loop(1, NK)
    def _(d):
        a2a(final, landed, o_send, o_recv, d).start()

    landed[k] = final[k]

    @pl.loop(1, NK)
    def _(d):
        a2a(final, landed, o_send, o_recv, d).wait_recv()

    for xy in range(8):
        cells = landed[:, xy * 8:xy * 8 + 8, :].reshape(MODES, MODES)
        out_ref[pl.ds(xy, MODES, stride=8), :] = jnp.transpose(cells)
    therm_ref[...] = jnp.sum(landed[:, 64:72, :], axis=0)

    @pl.loop(1, NK)
    def _(d):
        a2a(sent, state, in_send, in_recv, d).wait_send()
        a2a(final, landed, o_send, o_recv, d).wait_send()

    for link in ("x", "z"):
        for sg in (1, -1):
            for item in SLOTS:
                gcopy(link, sg, item).wait_send()
    for copy in core_copies:
        copy.wait_send()
    for t in range(ITERS):
        for way in range(2):
            xcopy(t, way).wait_send()
            zcopy(t, way).wait_send()


def shards(occupation, offset, warmth, courant, sign, matrix):
    f32, bf16 = jnp.float32, jnp.bfloat16
    dma = pltpu.SemaphoreType.DMA
    vmem = pl.BlockSpec(memory_space=pltpu.VMEM)
    out, therm = pl.pallas_call(
        kernel,
        out_shape=(
            jax.ShapeDtypeStruct((8 * MODES, 128), f32),
            jax.ShapeDtypeStruct((8, 128), f32),
        ),
        in_specs=[vmem] * 5 + [pl.BlockSpec(memory_space=pl.ANY)],
        out_specs=(vmem, vmem),
        scratch_shapes=[
            pltpu.VMEM((NA, NB, 8, 16, M), bf16),
            pltpu.VMEM((NK, 72, MODES), f32),
            pltpu.VMEM((NK, 72, MODES), f32),
            pltpu.VMEM((NK, 72, MODES), f32),
            pltpu.VMEM((NK, 72, MODES), f32),
            pltpu.VMEM((64, M), bf16),
            pltpu.VMEM((16, M), bf16),
            pltpu.VMEM((NK, 8, MODES), f32),
            pltpu.VMEM((ITERS, 2, NK, 32, MODES), bf16),
            pltpu.VMEM((ITERS, 2, NK, 32, MODES), bf16),
            pltpu.VMEM((ITERS, 2, NK, 8, MODES), f32),
            pltpu.VMEM((ITERS, 2, NK, 8, MODES), f32),
            pltpu.VMEM((NK, 64, MODES), f32),
            dma,
            dma((4, 15)), dma((4, 15)),
            dma((4, 6)), dma((4, 6)),
            dma((NK,)), dma((NK,)),
            dma((ITERS, 2)), dma((ITERS, 2)),
            dma((ITERS, 2)), dma((ITERS, 2)),
            dma((NK,)), dma((NK,)),
        ],
        compiler_params=pltpu.CompilerParams(
            collective_id=0, has_side_effects=True, vmem_limit_bytes=48 * 1024 * 1024
        ),
        cost_estimate=pl.CostEstimate(flops=1_700_000_000, bytes_accessed=2_000_000, transcendentals=0),
    )(
        occupation.reshape(8 * MODES, 128),
        offset.reshape(8, 128),
        warmth.reshape(NK, MODES),
        courant,
        sign.reshape(1, MODES),
        matrix.reshape(8, 16, M),
    )
    return out.reshape(occupation.shape), therm.reshape(offset.shape)


def solution(mesh):
    placed = (
        P("mode", "space", None, None),
        P("space", None, None),
        P(),
        P(None, "mode"),
        P("mode"),
        P("mode", None),
    )
    return jax.shard_map(
        shards,
        mesh=mesh,
        in_specs=placed,
        out_specs=(P("mode", "space", None, None), P("space", None, None)),
        check_vma=False,
    )
```

time: 314 us -> 201 us (0.64)
  the two profiles are of different devices: /device:TPU:16 before, /device:TPU:6 now
where the time goes in v1:
time: 201 us; the launch traced here: 200 us
  Pallas kernels  194 us (97%)
  local copies, waits for them, and re-layouts  5.52 us (3%)
    pallas_call x1, Pallas kernels, shards(): pl.pallas_call(kernel, out_shape=(jax.ShapeDtypeStruct((8 * MODES, 128),...  194 us
    unnamed x14, local copies, waits for them, and re-layouts  5.52 us

profile of v1, /device:TPU:6, one launch (start us, length us, event | category | flops | bytes accessed | tf_op | source)
XLA Modules:
  0.0 200.4 jit_solution(10929099856988216734)
XLA Ops:
  0.6 0.0 copy-start.2
  0.6 0.0 copy-start.5
  0.7 0.7 copy-done.2
  1.3 0.0 copy-done.5
  1.3 0.0 copy-start
  1.3 1.0 copy-done
  2.4 0.0 copy-start.1
  2.4 1.0 copy-done.1
  3.4 0.0 copy-start.3
  3.4 0.7 copy-done.3
  4.1 0.0 copy-start.4
  4.1 0.7 copy-done.4
  4.8 194.3 %shard_map.77 = (f32[1024,128]{1,0:T(8,128)S(1)}, f32[8,128]{1,0:T(8,128)S(1)}) custom-call(f32[1024,128]{1,0:T(8,128)S(1)} %bitcast.9, f32[8,128]{1,0:T(8,128)S(1)} %bitcast.12, f32[16,128]{1,0:T(8,128)S(1)} %bitcast.11, f32[3,128]{1,0:T(4,128)S(1)} %copy-done.4, s32[1,128]{1,0:T(1,128)S(1)} %bitcast.13, bf16[8,16,2048]{2,1,0:T(8,128)(2,1)S(1)} %bitcast.10), custom_call_target="tpu_custom_call" | custom-call | flops 1700000000 | bytes 2000000 | tf_op jit(solution)/shard_map/pallas_call | solution.py:333
  199.0 0.8 copy.10
  199.8 0.6 copy.11
Async XLA Ops:
  0.6 0.7 copy-start.2
  0.6 0.7 copy-start.5
  1.3 1.0 copy-start
  2.4 1.0 copy-start.1
  3.4 0.7 copy-start.3
  4.1 0.7 copy-start.4

commit v2 on v1

--- a/solution.py
+++ b/solution.py
@@ -15,18 +15,11 @@
 M = NK * MODES
 MESH = pl.DeviceIdType.MESH
 
-SLOTS = [
-    ("p", 0), ("r", 0, 0), ("p", 1), ("r", 0, 1), ("p", 2), ("r", 0, 2), ("r", 1, 0), ("r", 0, 3),
-    ("r", 1, 1), ("r", 1, 2), ("r", 2, 0), ("r", 1, 3), ("r", 2, 1), ("r", 2, 2), ("r", 2, 3),
-]
-SEQ = {item: n for n, item in enumerate(SLOTS)}
-
-
 def kernel(
     occ_ref, t0_ref, warm_ref, cour_ref, sign_ref, s_ref,
     out_ref, therm_ref,
     full, sent, state, final, landed, lhs, wlhs, relax, xs, xr, zs, zr, moved,
-    own_sem, g_send, g_recv, c_send, c_recv, in_send, in_recv, x_send, x_recv, z_send, z_recv, o_send, o_recv,
+    own_sem, gz_send, gz_recv, gx_send, gx_recv, gy_send, gy_recv, c_send, c_recv, in_send, in_recv, x_send, x_recv, z_send, z_recv, o_send, o_recv,
 ):
     s = lax.axis_index("space")
     k = lax.axis_index("mode")
@@ -40,13 +33,16 @@
     def wrap(v, n):
         return lax.rem(v + 4 * n, n)
 
-    def x_peer(sg):
-        return dev(s, a * NB + wrap(b + sg, NB))
-
-    def z_peer(sg):
-        crosses = lo if sg > 0 else 1 - lo
-        return dev(lax.rem(s + 16, NS), wrap(a + sg * crosses, NA) * NB + b)
-
+    y = (s // 2) % 8
+    toward = 2 * lo - 1
+    z_peers = (
+        dev(lax.rem(s + 16, NS), wrap(a + toward, NA) * NB + b),
+        dev(s, wrap(a + toward, NA) * NB + b),
+        dev(lax.rem(s + 16, NS), wrap(a + 2, NA) * NB + b),
+    )
+    x_up, x_down = dev(s, a * NB + wrap(b + 1, NB)), dev(s, a * NB + wrap(b - 1, NB))
+    y_up = dev(lo * 16 + wrap(y + 1, 8) * 2 + core, k)
+    y_down = dev(lo * 16 + wrap(y - 1, 8) * 2 + core, k)
     partner = dev(s + 1 - 2 * core, k)
     right, left = dev(wrap(s + 1, NS), k), dev(wrap(s - 1, NS), k)
     z_next, z_prev = dev(s, wrap(k + 1, NK)), dev(s, wrap(k - 1, NK))
@@ -62,7 +58,7 @@
     def _(d):
         pl.semaphore_signal(barrier, inc=1, device_id=dev(s, mode_peer(d)), device_id_type=MESH)
 
-    for peer in (right, left, z_peer(1), z_peer(-1)):
+    for peer in (right, left, z_peers[0], z_peers[2], y_up, y_down):
         pl.semaphore_signal(barrier, inc=1, device_id=peer, device_id_type=MESH)
 
     warm_col = jnp.transpose(jnp.broadcast_to(warm_ref[pl.ds(k, 1), :], (MODES, MODES)))
@@ -79,7 +75,7 @@
         coef = jnp.where(row == 2 * d + 1, jnp.where(bit == 1, c, 0.0), coef)
     sent[:, 64:72, :] = jnp.broadcast_to(coef[None], (NK, 8, MODES))
 
-    pl.semaphore_wait(barrier, NK - 1 + 4)
+    pl.semaphore_wait(barrier, NK - 1 + 6)
 
     def a2a(src, dst, send, recv, d):
         there = mode_peer(d)
@@ -88,118 +84,78 @@
             device_id=dev(s, there), device_id_type=MESH,
         )
 
+    own.wait()
+    rows = [a, wrap(a + toward, NA), wrap(a - toward, NA), wrap(a + 2, NA)]
+    cols = [b, wrap(b - 1, NB), wrap(b + 1, NB), wrap(b + 2, NB)]
+    mine_u = (y % 2) * 4 + core * 2
+    other_u = (1 - y % 2) * 4 + core * 2
+    started = []
+
+    def remote(block, send, recv, peer):
+        return pltpu.make_async_remote_copy(
+            src_ref=block, dst_ref=block, send_sem=send, recv_sem=recv, device_id=peer, device_id_type=MESH
+        )
+
+    def z_copy(n):
+        return remote(full.at[a, b, pl.ds(mine_u, 2)], gz_send.at[n], gz_recv.at[n], z_peers[n - 1])
+
+    def x_copy(n, step):
+        if step < 2:
+            block = full.at[rows[n], b, pl.ds(mine_u, 2)]
+        else:
+            block = full.at[rows[n], cols[step - 1], mine_u + step - 2]
+        return remote(block, gx_send.at[n, step], gx_recv.at[n, step], x_down if step % 2 else x_up)
+
+    def y_copy(n, m, way):
+        block = full.at[rows[n], cols[m], mine_u + way]
+        return remote(block, gy_send.at[n, m, way], gy_recv.at[n, m, way], y_down if way else y_up)
+
+    def core_copy(n, m, kind):
+        block = full.at[rows[n], cols[m], pl.ds(other_u if kind else mine_u, 2)]
+        return remote(block, c_send.at[n, m, kind], c_recv.at[n, m, kind], partner)
+
+    def start(copy):
+        copy.start()
+        started.append(copy)
+
+    def share(n, m):
+        start(y_copy(n, m, 0))
+        start(y_copy(n, m, 1))
+        start(core_copy(n, m, 0))
+
+    for n in range(1, 4):
+        start(z_copy(n))
+    start(x_copy(0, 0))
+    start(x_copy(0, 1))
+
     @pl.loop(1, NK)
     def _(d):
         a2a(sent, state, in_send, in_recv, d).start()
 
     state[k] = sent[k]
 
-    own.wait()
-
-    def piece(link, sg, item):
-        color = (0 if sg > 0 else 1) if (link == "x") == (item[0] == "r") else (2 if sg > 0 else 3)
-        return color
-
-    def z_from(sg, i):
-        follows = (1 - lo) if sg > 0 else lo
-        return wrap(a - sg * (i + follows), NA)
-
-    def x_from(sg, i):
-        return wrap(b - sg * i, NB)
-
-    def gcopy(link, sg, item):
-        li = (0 if link == "x" else 2) + (0 if sg > 0 else 1)
-        n = SEQ[item]
-        color = piece(link, sg, item)
-        i = item[1]
-        if link == "x":
-            row_ = a if item[0] == "p" else wrap(a - sg * item[2], NA)
-            at = (row_, x_from(sg, i))
-            peer = x_peer(sg)
-        else:
-            col_ = b if item[0] == "p" else wrap(b - sg * item[2], NB)
-            at = (z_from(sg, i), col_)
-            peer = z_peer(sg)
-        block = full.at[at[0], at[1], core * 4 + color]
-        return pltpu.make_async_remote_copy(
-            src_ref=block, dst_ref=block, send_sem=g_send.at[li, n], recv_sem=g_recv.at[li, n],
-            device_id=peer, device_id_type=MESH,
-        )
-
-    waited = set()
-
-    def wait_recv(link, sg, item):
-        if (link, sg, item) not in waited:
-            waited.add((link, sg, item))
-            gcopy(link, sg, item).wait_recv()
-
-    def leads(sg):
-        return lo == (1 if sg > 0 else 0)
-
-    core_copies = []
-
-    def core_copy(color, n, block):
-        copy = pltpu.make_async_remote_copy(
-            src_ref=block, dst_ref=block, send_sem=c_send.at[color, n], recv_sem=c_recv.at[color, n],
-            device_id=partner, device_id_type=MESH,
-        )
-        copy.start()
-        core_copies.append(copy)
-
-    def issue(link, sg, item):
-        other = "z" if link == "x" else "x"
-        i = item[1]
-        if item[0] == "r" and item[2] > 0:
-            wait_recv(other, sg, ("p", item[2] - 1))
-        before = (item[0], i - 1, *item[2:]) if i > 0 else None
-        if link == "x":
-            if before:
-                wait_recv(link, sg, before)
-            gcopy(link, sg, item).start()
-        else:
-            if before:
-                wait_recv(link, sg, before)
-            first = leads(sg)
-
-            @pl.when(first)
-            def _():
-                gcopy(link, sg, item).start()
-
-            @pl.when(jnp.logical_not(first))
-            def _():
-                gcopy(link, sg, item).wait_recv()
-                gcopy(link, sg, item).start()
-
-    def wait_recv(link, sg, item):
-        if (link, sg, item) in waited:
-            return
-        waited.add((link, sg, item))
-        if link == "x":
-            gcopy(link, sg, item).wait_recv()
-        else:
-            @pl.when(leads(sg))
-            def _():
-                gcopy(link, sg, item).wait_recv()
-
-    for item in SLOTS:
-        for link in ("x", "z"):
-            for sg in (1, -1):
-                issue(link, sg, item)
-        if item == ("r", 0, 3):
-            pass
-
-    for link in ("x", "z"):
-        for sg in (1, -1):
-            for item in SLOTS:
-                wait_recv(link, sg, item)
-    for sg in (1, -1):
-        cx, cz = (0, 2) if sg > 0 else (1, 3)
-        for q in range(1, 4):
-            core_copy(cx, q - 1, full.at[wrap(a - sg * q, NA), b, core * 4 + cx])
-            core_copy(cz, q - 1, full.at[a, wrap(b - sg * q, NB), core * 4 + cz])
-        for i in range(3):
-            core_copy(cx, 3 + i, full.at[:, wrap(b - sg * (i + 1), NB), core * 4 + cx])
-            core_copy(cz, 3 + i, full.at[wrap(a - sg * (i + 1), NA), :, core * 4 + cz])
+    for n in range(7):
+        if 0 < n < 4:
+            z_copy(n).wait_recv()
+            start(x_copy(n, 0))
+            start(x_copy(n, 1))
+            share(n, 0)
+        if 0 <= n - 1 < 4:
+            for m in (1, 2):
+                x_copy(n - 1, m - 1).wait_recv()
+                start(x_copy(n - 1, m + 1))
+            share(n - 1, 1)
+            share(n - 1, 2)
+        if 0 <= n - 2 < 4:
+            x_copy(n - 2, 2).wait_recv()
+            x_copy(n - 2, 3).wait_recv()
+            share(n - 2, 3)
+        if 0 <= n - 3 < 4:
+            for m in range(4):
+                if n - 3 or m:
+                    y_copy(n - 3, m, 0).wait_recv()
+                    y_copy(n - 3, m, 1).wait_recv()
+                    start(core_copy(n - 3, m, 1))
 
     @pl.loop(1, NK)
     def _(d):
@@ -270,14 +226,23 @@
         thermal = jnp.broadcast_to(thermal, (64, MODES))
 
         if t == 0:
-            for copy in core_copies:
-                copy.wait_recv()
+            for n in range(4):
+                for m in range(4):
+                    if n or m:
+                        core_copy(n, m, 0).wait_recv()
+                        core_copy(n, m, 1).wait_recv()
 
         nt = (((1,), (1,)), ((), ()))
-        target = final if t == ITERS - 1 else state
+        last = t == ITERS - 1
+        target = final if last else state
+        if last:
+            lane = lax.broadcasted_iota(jnp.int32, (8, 8, MODES), 2)
+            mine = jnp.sum(jnp.where(lane == 8 * k + zi, thermal.reshape(8, 8, MODES), 0.0), axis=1)
+            final[:, 64:72, :] = jnp.broadcast_to(mine[None], (NK, 8, MODES))
 
         @pl.loop(0, NK // 2)
-        def _(n):
+        def _(step):
+            n = lax.rem(k // 2 + step, NK // 2)
             w = full[n // 2, pl.ds((n % 2) * 2, 2)].reshape(2 * MODES, M)
             product = lax.dot_general(lhs[...], w, nt, preferred_element_type=jnp.float32)
             if t == 0:
@@ -289,14 +254,12 @@
                 j = 2 * n + h
                 pr = product[:, h * MODES:(h + 1) * MODES]
                 target[j, 0:64, :] = moved[j] - pr + relax[j, 0:1] * thermal
-
-    lane = lax.broadcasted_iota(jnp.int32, (8, 8, MODES), 2)
-    mine = jnp.sum(jnp.where(lane == 8 * k + zi, thermal.reshape(8, 8, MODES), 0.0), axis=1)
-    final[:, 64:72, :] = jnp.broadcast_to(mine[None], (NK, 8, MODES))
-
-    @pl.loop(1, NK)
-    def _(d):
-        a2a(final, landed, o_send, o_recv, d).start()
+                if last:
+                    d = lax.rem(j - k + NK, NK)
+
+                    @pl.when(d > 0)
+                    def _():
+                        a2a(final, landed, o_send, o_recv, d).start()
 
     landed[k] = final[k]
 
@@ -314,11 +277,7 @@
         a2a(sent, state, in_send, in_recv, d).wait_send()
         a2a(final, landed, o_send, o_recv, d).wait_send()
 
-    for link in ("x", "z"):
-        for sg in (1, -1):
-            for item in SLOTS:
-                gcopy(link, sg, item).wait_send()
-    for copy in core_copies:
+    for copy in started:
         copy.wait_send()
     for t in range(ITERS):
         for way in range(2):
@@ -353,8 +312,10 @@
             pltpu.VMEM((ITERS, 2, NK, 8, MODES), f32),
             pltpu.VMEM((NK, 64, MODES), f32),
             dma,
-            dma((4, 15)), dma((4, 15)),
-            dma((4, 6)), dma((4, 6)),
+            dma((4,)), dma((4,)),
+            dma((4, 4)), dma((4, 4)),
+            dma((4, 4, 2)), dma((4, 4, 2)),
+            dma((4, 4, 2)), dma((4, 4, 2)),
             dma((NK,)), dma((NK,)),
             dma((ITERS, 2)), dma((ITERS, 2)),
             dma((ITERS, 2)), dma((ITERS, 2)),

time: 201 us -> 107 us (0.53)
  the two profiles are of different devices: /device:TPU:6 before, /device:TPU:15 now
where the time goes in v2:
time: 107 us
  Pallas kernels  101 us (94%)
  local copies, waits for them, and re-layouts  5.52 us (5%)
    pallas_call x1, Pallas kernels, shards(): pl.pallas_call(kernel, out_shape=(jax.ShapeDtypeStruct((8 * MODES, 128),...  101 us
    unnamed x14, local copies, waits for them, and re-layouts  5.52 us

profile of v2, /device:TPU:15, one launch (start us, length us, event | category | flops | bytes accessed | tf_op | source)
XLA Modules:
  0.0 106.8 jit_solution(17846267588357187314)
XLA Ops:
  0.6 0.0 copy-start.2
  0.6 0.0 copy-start.5
  0.7 0.7 copy-done.2
  1.3 0.0 copy-done.5
  1.3 0.0 copy-start
  1.3 1.0 copy-done
  2.4 0.0 copy-start.1
  2.4 1.0 copy-done.1
  3.4 0.0 copy-start.3
  3.4 0.7 copy-done.3
  4.1 0.0 copy-start.4
  4.1 0.7 copy-done.4
  4.8 100.6 %shard_map.77 = (f32[1024,128]{1,0:T(8,128)S(1)}, f32[8,128]{1,0:T(8,128)S(1)}) custom-call(f32[1024,128]{1,0:T(8,128)S(1)} %bitcast.9, f32[8,128]{1,0:T(8,128)S(1)} %bitcast.12, f32[16,128]{1,0:T(8,128)S(1)} %bitcast.11, f32[3,128]{1,0:T(4,128)S(1)} %copy-done.4, s32[1,128]{1,0:T(1,128)S(1)} %bitcast.13, bf16[8,16,2048]{2,1,0:T(8,128)(2,1)S(1)} %bitcast.10), custom_call_target="tpu_custom_call" | custom-call | flops 1700000000 | bytes 2000000 | tf_op jit(solution)/shard_map/pallas_call | solution.py:292
  105.4 0.8 copy.10
  106.2 0.6 copy.11
Async XLA Ops:
  0.6 0.7 copy-start.2
  0.6 0.7 copy-start.5
  1.3 1.0 copy-start
  2.4 1.0 copy-start.1
  3.4 0.7 copy-start.3
  4.1 0.7 copy-start.4

commit v3 on v2

v3 whole, which is shorter than its diff:
```python
import functools

import jax
import jax.numpy as jnp
from jax import lax
from jax.experimental import pallas as pl
from jax.experimental.pallas import tpu as pltpu
from jax.sharding import PartitionSpec as P

ITERS = 3
NA, NB = 4, 4
NK = NA * NB
NS = 32
MODES = 128
M = NK * MODES
MESH = pl.DeviceIdType.MESH

def kernel(
    occ_hbm, t0_hbm, warm_hbm, cour_hbm, sign_hbm, s_hbm,
    out_ref, therm_ref,
    occ_ref, t0_ref, warm_ref, cour_ref, sign_ref,
    full, sent, state, q_sent, q_state, coef_sent, coefs, q_final, q_landed, tail, tails, back, lhs, wlhs, relax, xs, xr, zs, zr, moved, half,
    fetch_sem, own_sem, gz_send, gz_recv, gx_send, gx_recv, gy_send, gy_recv, c_send, c_recv, in_send, in_recv, x_send, x_recv, z_send, z_recv, o_send, o_recv,
):
    s = lax.axis_index("space")
    k = lax.axis_index("mode")
    a, b = k // NB, k % NB
    lo = s // 16
    core = s % 2

    def dev(space, mode):
        return {"space": space, "mode": mode}

    def wrap(v, n):
        return lax.rem(v + 4 * n, n)

    y = (s // 2) % 8
    toward = 2 * lo - 1
    z_peers = (
        dev(lax.rem(s + 16, NS), wrap(a + toward, NA) * NB + b),
        dev(s, wrap(a + toward, NA) * NB + b),
        dev(lax.rem(s + 16, NS), wrap(a + 2, NA) * NB + b),
    )
    x_up, x_down = dev(s, a * NB + wrap(b + 1, NB)), dev(s, a * NB + wrap(b - 1, NB))
    y_up = dev(lo * 16 + wrap(y + 1, 8) * 2 + core, k)
    y_down = dev(lo * 16 + wrap(y - 1, 8) * 2 + core, k)
    partner = dev(s + 1 - 2 * core, k)
    right, left = dev(wrap(s + 1, NS), k), dev(wrap(s - 1, NS), k)
    z_next, z_prev = dev(s, wrap(k + 1, NK)), dev(s, wrap(k - 1, NK))

    def mode_peer(d):
        return wrap(k + d, NK)

    fetches = [
        pltpu.make_async_copy(src, dst, fetch_sem.at[i])
        for i, (src, dst) in enumerate((
            (occ_hbm, occ_ref), (t0_hbm, t0_ref), (warm_hbm, warm_ref), (cour_hbm, cour_ref), (sign_hbm, sign_ref),
        ))
    ]
    for fetch in fetches:
        fetch.start()
    own = pltpu.make_async_copy(s_hbm, full.at[a, b], own_sem)
    own.start()
    barrier = pltpu.get_barrier_semaphore()

    @pl.loop(1, NK)
    def _(d):
        pl.semaphore_signal(barrier, inc=1, device_id=dev(s, mode_peer(d)), device_id_type=MESH)

    for peer in (right, left, z_peers[0], z_peers[2], y_up, y_down):
        pl.semaphore_signal(barrier, inc=1, device_id=peer, device_id_type=MESH)

    pl.semaphore_wait(barrier, NK - 1 + 6)

    own.wait()
    rows = [a, wrap(a + toward, NA), wrap(a - toward, NA), wrap(a + 2, NA)]
    cols = [b, wrap(b - 1, NB), wrap(b + 1, NB), wrap(b + 2, NB)]
    mine_u = (y % 2) * 4 + core * 2
    other_u = (1 - y % 2) * 4 + core * 2
    started = []

    def remote(block, send, recv, peer):
        return pltpu.make_async_remote_copy(
            src_ref=block, dst_ref=block, send_sem=send, recv_sem=recv, device_id=peer, device_id_type=MESH
        )

    def z_copy(n, kind):
        block = full.at[a, b, pl.ds(other_u if kind else mine_u, 2)]
        return remote(block, gz_send.at[n, kind], gz_recv.at[n, kind], z_peers[n - 1])

    def x_copy(n, step, kind=0):
        if step < 2:
            block = full.at[rows[n], b, pl.ds(other_u if kind else mine_u, 2)]
        else:
            block = full.at[rows[n], cols[step - 1], mine_u + step - 2]
        return remote(block, gx_send.at[n, step, kind], gx_recv.at[n, step, kind], x_down if step % 2 else x_up)

    def y_copy(n, m, way):
        block = full.at[rows[n], cols[m], mine_u + way]
        return remote(block, gy_send.at[n, m, way], gy_recv.at[n, m, way], y_down if way else y_up)

    def core_copy(n, m, kind):
        block = full.at[rows[n], cols[m], pl.ds(other_u if kind else mine_u, 2)]
        return remote(block, c_send.at[n, m, kind], c_recv.at[n, m, kind], partner)

    def start(copy):
        copy.start()
        started.append(copy)

    def whole(n, m):
        return (n, m) in ((0, 0), (0, 1), (0, 2), (1, 0))

    def share(n, m):
        if not whole(n, m):
            start(y_copy(n, m, 0))
            start(y_copy(n, m, 1))
        start(core_copy(n, m, 0))

    start(z_copy(1, 0))
    start(x_copy(0, 0))
    start(x_copy(0, 1))
    start(z_copy(2, 0))
    start(z_copy(3, 0))
    start(x_copy(0, 0, 1))
    start(x_copy(0, 1, 1))
    start(z_copy(1, 1))

    def a2a(src, dst, extra, extra_dst, send, recv, d):
        there = mode_peer(d)
        return [
            pltpu.make_async_remote_copy(
                src_ref=s_.at[there], dst_ref=d_.at[k], send_sem=send.at[d, i], recv_sem=recv.at[d, i],
                device_id=dev(s, there), device_id_type=MESH,
            )
            for i, (s_, d_) in enumerate(((src, dst), (extra, extra_dst)))
        ]

    def a2a_in(d):
        return a2a(q_sent, q_state, coef_sent, coefs, in_send, in_recv, d)

    def a2a_out(d):
        return a2a(q_final, q_landed, tail, tails, o_send, o_recv, d)

    def quantized(values):
        most = jnp.max(jnp.abs(values), axis=0, keepdims=True)
        steps = jnp.where(most > 0.0, 32767.0 / most, 0.0)
        return jnp.round(values * steps).astype(jnp.int32).astype(jnp.int16), most * (1.0 / 32767.0)

    def restored(q, step):
        return q.astype(jnp.int32).astype(jnp.float32) * step

    for fetch in fetches:
        fetch.wait()

    warm_col = jnp.transpose(jnp.broadcast_to(warm_ref[pl.ds(k, 1), :], (MODES, MODES)))
    for xy in range(8):
        cells = occ_ref[pl.ds(xy, MODES, stride=8), :] + warm_col * t0_ref[xy:xy + 1, :]
        sent[:, pl.ds(xy * 8, 8), :] = jnp.transpose(cells).reshape(NK, 8, MODES)
    sign = sign_ref[...]
    row = lax.broadcasted_iota(jnp.int32, (8, MODES), 0)
    coef = jnp.zeros((8, MODES), jnp.float32)
    for d in range(3):
        bit = jnp.broadcast_to((sign >> d) & 1, (8, MODES))
        c = jnp.broadcast_to(cour_ref[d:d + 1, :], (8, MODES))
        coef = jnp.where(row == 2 * d, jnp.where(bit == 0, c, 0.0), coef)
        coef = jnp.where(row == 2 * d + 1, jnp.where(bit == 1, c, 0.0), coef)

    @pl.loop(0, NK)
    def _(j):
        q, step = quantized(sent[j])
        q_sent[j] = q
        coef_sent[j] = jnp.where(row == 6, jnp.broadcast_to(step, (8, MODES)), coef)

    @pl.loop(1, NK)
    def _(d):
        for copy in a2a_in(d):
            copy.start()

    q_state[k] = q_sent[k]
    coefs[k] = coef_sent[k]

    def gather_stage(n):
        if 0 < n < 4:
            z_copy(n, 0).wait_recv()
            start(x_copy(n, 0))
            start(x_copy(n, 1))
            share(n, 0)
        if 0 <= n - 1 < 4:
            for m in (1, 2):
                x_copy(n - 1, m - 1).wait_recv()
                start(x_copy(n - 1, m + 1))
            share(n - 1, 1)
            share(n - 1, 2)
        if 0 <= n - 2 < 4:
            x_copy(n - 2, 2).wait_recv()
            x_copy(n - 2, 3).wait_recv()
            share(n - 2, 3)
        if 0 <= n - 3 < 4:
            for m in range(4):
                if n - 3 or m:
                    if not whole(n - 3, m):
                        y_copy(n - 3, m, 0).wait_recv()
                        y_copy(n - 3, m, 1).wait_recv()
                    elif m:
                        x_copy(0, m - 1, 1).wait_recv()
                    else:
                        z_copy(1, 1).wait_recv()
                    start(core_copy(n - 3, m, 1))

    for n in range(4):
        gather_stage(n)

    total = jnp.sum(warm_ref[...])
    zi = lax.broadcasted_iota(jnp.int32, (8, 8, MODES), 1)
    nt = (((1,), (1,)), ((), ()))
    H = NK // 2

    def halo_copies(t, h):
        part = pl.ds(h * H, H)
        return [
            pltpu.make_async_remote_copy(
                src_ref=src.at[t, way, part], dst_ref=dst.at[t, way, part],
                send_sem=send.at[t, way, h], recv_sem=recv.at[t, way, h], device_id=peer, device_id_type=MESH,
            )
            for src, dst, send, recv, peers in (
                (xs, xr, x_send, x_recv, (right, left)), (zs, zr, z_send, z_recv, (z_next, z_prev)),
            )
            for way, peer in enumerate(peers)
        ]

    def stage_halo(t, j):
        xs[t, 0, j] = state[j, 32:64, :].astype(jnp.bfloat16)
        xs[t, 1, j] = state[j, 0:32, :].astype(jnp.bfloat16)
        zs[t, 0, j] = state[j, pl.ds(7, 8, stride=8), :]
        zs[t, 1, j] = state[j, pl.ds(0, 8, stride=8), :]

    def send_halo(t, h):
        for copy in halo_copies(t, h):
            copy.start()

    def advect_block(t, j, energy):
        st = state[j].reshape(8, 8, MODES)
        cf = [coefs[j, pl.ds(r, 1), :].reshape(1, 1, MODES) for r in range(6)]
        below = xr[t, 0, j].astype(jnp.float32).reshape(4, 8, MODES)
        above = xr[t, 1, j].astype(jnp.float32).reshape(4, 8, MODES)
        x_below = jnp.concatenate([below, st[0:4]], axis=0)
        x_above = jnp.concatenate([st[4:8], above], axis=0)
        y_below = jnp.concatenate([st[3:4], st[0:3], st[7:8], st[4:7]], axis=0)
        y_above = jnp.concatenate([st[1:4], st[0:1], st[5:8], st[4:5]], axis=0)
        z_lower = zr[t, 0, j].reshape(8, 1, MODES)
        z_upper = zr[t, 1, j].reshape(8, 1, MODES)
        z_below = jnp.where(zi == 0, z_lower, jnp.roll(st, 1, 1))
        z_above = jnp.where(zi == 7, z_upper, jnp.roll(st, -1, 1))
        mv = st
        for d, (lower, upper) in enumerate(((x_below, x_above), (y_below, y_above), (z_below, z_above))):
            mv = mv - (cf[2 * d] * (st - lower) + cf[2 * d + 1] * (st - upper))
        mv = mv.reshape(64, MODES)
        mv_bf = mv.astype(jnp.bfloat16)
        moved[j] = mv
        lhs[:, pl.ds(pl.multiple_of(j * MODES, MODES), MODES)] = mv_bf
        return energy + mv_bf.astype(jnp.float32) * warm_ref[pl.ds(j, 1), :]

    def advect(t, h, energy):
        for copy in halo_copies(t, h):
            copy.wait_recv()
        return lax.fori_loop(h * H, h * H + H, functools.partial(advect_block, t), energy)

    def offset(energy):
        thermal = jnp.sum(energy, axis=1, keepdims=True) / total
        return jnp.broadcast_to(thermal, (64, MODES))

    nothing = jnp.zeros((64, MODES), jnp.float32)

    row16 = lax.broadcasted_iota(jnp.int32, (16, MODES), 0)
    for j in range(NK):
        w = jnp.broadcast_to(warm_ref[j:j + 1, :], (16, MODES))
        hi = w.astype(jnp.bfloat16).astype(jnp.float32)
        mid = (w - hi).astype(jnp.bfloat16).astype(jnp.float32)
        low = w - hi - mid
        parts = jnp.where(row16 == 0, hi, jnp.where(row16 == 1, mid, jnp.where(row16 == 2, low, 0.0)))
        wlhs[:, j * MODES:(j + 1) * MODES] = parts.astype(jnp.bfloat16)

    @pl.loop(1, NK)
    def _(d):
        for copy in a2a_in(d):
            copy.wait_recv()

    for h in range(2):
        @pl.loop(h * H, h * H + H)
        def _(j):
            state[j] = restored(q_state[j], coefs[j, 6:7])
            stage_halo(0, j)

        send_halo(0, h)

    gather_stage(4)
    gather_stage(5)
    thermal = offset(advect(0, 1, advect(0, 0, nothing)))
    gather_stage(6)

    for n in range(4):
        for m in range(4):
            if n or m:
                core_copy(n, m, 0).wait_recv()
                core_copy(n, m, 1).wait_recv()

        @pl.loop(0, 2)
        def _(pair):
            r = rows[n]
            w = full[r, pl.ds(pair * 2, 2)].reshape(2 * MODES, M)
            product = lax.dot_general(lhs[...], w, nt, preferred_element_type=jnp.float32)
            parts = lax.dot_general(wlhs[...], w, nt, preferred_element_type=jnp.float32)
            both = parts[0:1] + parts[1:2] + parts[2:3]
            for e in range(2):
                j = r * NB + pair * 2 + e
                rx = jnp.broadcast_to(both[:, e * MODES:(e + 1) * MODES], (8, MODES))
                relax[j] = rx
                state[j] = moved[j] - product[:, e * MODES:(e + 1) * MODES] + rx[0:1] * thermal
                stage_halo(1, j)

    for h in range(2):
        send_halo(1, h)

    for t in range(1, ITERS):
        last = t == ITERS - 1
        energy = advect(t, 0, nothing)

        @pl.loop(0, H)
        def _(n):
            w = full[n // 2, pl.ds((n % 2) * 2, 2), :, :, 0:M // 2].reshape(2 * MODES, M // 2)
            half[n] = lax.dot_general(lhs[:, 0:M // 2], w, nt, preferred_element_type=jnp.float32)

        thermal = offset(advect(t, 1, energy))
        if last:
            lane = lax.broadcasted_iota(jnp.int32, (8, 8, MODES), 2)
            mine = jnp.sum(jnp.where(lane == 8 * k + zi, thermal.reshape(8, 8, MODES), 0.0), axis=1)
            tail[:, 0:8, :] = jnp.broadcast_to(mine[None], (NK, 8, MODES))

        def finish(n):
            w = full[n // 2, pl.ds((n % 2) * 2, 2), :, :, M // 2:M].reshape(2 * MODES, M // 2)
            product = half[n] + lax.dot_general(lhs[:, M // 2:M], w, nt, preferred_element_type=jnp.float32)
            for e in range(2):
                j = 2 * n + e
                new = moved[j] - product[:, e * MODES:(e + 1) * MODES] + relax[j, 0:1] * thermal
                if last:
                    q, step = quantized(new)
                    q_final[j] = q
                    tail[j, 8:16, :] = jnp.broadcast_to(step, (8, MODES))
                    d = lax.rem(j - k + NK, NK)

                    @pl.when(d > 0)
                    def _():
                        for copy in a2a_out(d):
                            copy.start()
                else:
                    state[j] = new
                    stage_halo(t + 1, j)

        if last:
            @pl.loop(0, H)
            def _(step):
                finish(lax.rem(k // 2 + step, H))
        else:
            for h in range(2):
                @pl.loop(h * H // 2, (h + 1) * H // 2)
                def _(n):
                    finish(n)

                send_halo(t + 1, h)

    q_landed[k] = q_final[k]
    tails[k] = tail[k]

    @pl.loop(1, NK)
    def _(d):
        for copy in a2a_out(d):
            copy.wait_recv()

    @pl.loop(0, NK)
    def _(j):
        back[j] = restored(q_landed[j], tails[j, 8:9]).reshape(8, 8, MODES)

    for xy in range(8):
        cells = back[:, xy].reshape(MODES, MODES)
        out_ref[pl.ds(xy, MODES, stride=8), :] = jnp.transpose(cells)
    therm_ref[...] = jnp.sum(tails[:, 0:8, :], axis=0)

    @pl.loop(1, NK)
    def _(d):
        for copy in a2a_in(d) + a2a_out(d):
            copy.wait_send()

    for copy in started:
        copy.wait_send()
    for t in range(ITERS):
        for h in range(2):
            for copy in halo_copies(t, h):
                copy.wait_send()


def shards(occupation, offset, warmth, courant, sign, matrix):
    f32, bf16 = jnp.float32, jnp.bfloat16
    dma = pltpu.SemaphoreType.DMA
    vmem = pl.BlockSpec(memory_space=pltpu.VMEM)
    out, therm = pl.pallas_call(
        kernel,
        out_shape=(
            jax.ShapeDtypeStruct((8 * MODES, 128), f32),
            jax.ShapeDtypeStruct((8, 128), f32),
        ),
        in_specs=[pl.BlockSpec(memory_space=pltpu.HBM)] * 6,
        out_specs=(vmem, vmem),
        scratch_shapes=[
            pltpu.VMEM((8 * MODES, 128), f32),
            pltpu.VMEM((8, 128), f32),
            pltpu.VMEM((NK, MODES), f32),
            pltpu.VMEM((3, MODES), f32),
            pltpu.VMEM((1, MODES), jnp.int32),
            pltpu.VMEM((NA, NB, 8, 16, M), bf16),
            pltpu.VMEM((NK, 64, MODES), f32),
            pltpu.VMEM((NK, 64, MODES), f32),
            pltpu.VMEM((NK, 64, MODES), jnp.int16),
            pltpu.VMEM((NK, 64, MODES), jnp.int16),
            pltpu.VMEM((NK, 8, MODES), f32),
            pltpu.VMEM((NK, 8, MODES), f32),
            pltpu.VMEM((NK, 64, MODES), jnp.int16),
            pltpu.VMEM((NK, 64, MODES), jnp.int16),
            pltpu.VMEM((NK, 16, MODES), f32),
            pltpu.VMEM((NK, 16, MODES), f32),
            pltpu.VMEM((NK, 8, 8, MODES), f32),
            pltpu.VMEM((64, M), bf16),
            pltpu.VMEM((16, M), bf16),
            pltpu.VMEM((NK, 8, MODES), f32),
            pltpu.VMEM((ITERS, 2, NK, 32, MODES), bf16),
            pltpu.VMEM((ITERS, 2, NK, 32, MODES), bf16),
            pltpu.VMEM((ITERS, 2, NK, 8, MODES), f32),
            pltpu.VMEM((ITERS, 2, NK, 8, MODES), f32),
            pltpu.VMEM((NK, 64, MODES), f32),
            pltpu.VMEM((NK // 2, 64, 2 * MODES), f32),
            dma((5,)),
            dma,
            dma((4, 2)), dma((4, 2)),
            dma((4, 4, 2)), dma((4, 4, 2)),
            dma((4, 4, 2)), dma((4, 4, 2)),
            dma((4, 4, 2)), dma((4, 4, 2)),
            dma((NK, 2)), dma((NK, 2)),
            dma((ITERS, 2, 2)), dma((ITERS, 2, 2)),
            dma((ITERS, 2, 2)), dma((ITERS, 2, 2)),
            dma((NK, 2)), dma((NK, 2)),
        ],
        compiler_params=pltpu.CompilerParams(
            collective_id=0, has_side_effects=True, vmem_limit_bytes=62 * 1024 * 1024
        ),
        cost_estimate=pl.CostEstimate(flops=1_700_000_000, bytes_accessed=2_000_000, transcendentals=0),
    )(
        occupation.reshape(8 * MODES, 128),
        offset.reshape(8, 128),
        warmth.reshape(NK, MODES),
        courant,
        sign.reshape(1, MODES),
        matrix.reshape(8, 16, M),
    )
    return out.reshape(occupation.shape), therm.reshape(offset.shape)


def solution(mesh):
    placed = (
        P("mode", "space", None, None),
        P("space", None, None),
        P(),
        P(None, "mode"),
        P("mode"),
        P("mode", None),
    )
    return jax.shard_map(
        shards,
        mesh=mesh,
        in_specs=placed,
        out_specs=(P("mode", "space", None, None), P("space", None, None)),
        check_vma=False,
    )
```

time: 107 us -> 92.1 us (0.86)
  the two profiles are of different devices: /device:TPU:15 before, /device:TPU:6 now
where the time goes in v3:
time: 92.1 us; the launch traced here: 92 us
  Pallas kernels  88.8 us (96%)
  local copies, waits for them, and re-layouts  2.47 us (3%)
    pallas_call x1, Pallas kernels, shards(): pl.pallas_call(kernel, out_shape=(jax.ShapeDtypeStruct((8 * MODES, 128),...  88.8 us
    unnamed x4, local copies, waits for them, and re-layouts  2.47 us

profile of v3, /device:TPU:6, one launch (start us, length us, event | category | flops | bytes accessed | tf_op | source)
XLA Modules:
  0.0 92.0 jit_solution(11973479894908994480)
XLA Ops:
  0.6 88.8 %shard_map.77 = (f32[1024,128]{1,0:T(8,128)}, f32[8,128]{1,0:T(8,128)}) custom-call(f32[1024,128]{1,0:T(8,128)} %bitcast.9, f32[8,128]{1,0:T(8,128)} %bitcast.12, f32[16,128]{1,0:T(8,128)} %bitcast.11, f32[3,128]{1,0:T(4,128)} %cour_hbm.1, s32[1,128]{1,0:T(1,128)} %bitcast.13, bf16[8,16,2048]{2,1,0:T(8,128)(2,1)} %bitcast.10), custom_call_target="tpu_custom_call" | custom-call | flops 1700000000 | bytes 2000000 | tf_op jit(solution)/shard_map/pallas_call | solution.py:405
  89.5 0.0 copy-start
  89.5 1.9 %copy.10 = f32[128,2,4,128]{3,2,1,0:T(4,128)} copy(f32[128,2,4,128]{3,2,1,0:T(4,128)} %bitcast.7) | data formatting | bytes 1048576
  91.4 0.0 copy-done
  91.4 0.6 copy.11
Async XLA Ops:
  89.5 1.9 %copy-start = (f32[8,128]{1,0:T(8,128)S(1)}, f32[8,128]{1,0:T(8,128)}, u32[]{:S(2)}) copy-start(f32[8,128]{1,0:T(8,128)} %get-tuple-element.5) | copy-start | bytes 12292

commit v4 on v3

--- a/solution.py
+++ b/solution.py
@@ -17,10 +17,10 @@
 
 def kernel(
     occ_hbm, t0_hbm, warm_hbm, cour_hbm, sign_hbm, s_hbm,
-    out_ref, therm_ref,
+    q_landed, tails,
     occ_ref, t0_ref, warm_ref, cour_ref, sign_ref,
-    full, sent, state, q_sent, q_state, coef_sent, coefs, q_final, q_landed, tail, tails, back, lhs, wlhs, relax, xs, xr, zs, zr, moved, half,
-    fetch_sem, own_sem, gz_send, gz_recv, gx_send, gx_recv, gy_send, gy_recv, c_send, c_recv, in_send, in_recv, x_send, x_recv, z_send, z_recv, o_send, o_recv,
+    full, sent, state, q_sent, q_state, coef_sent, coefs, q_final, tail, lhs, wlhs, relax, xs, xr, zs, zr, moved, half,
+    fetch_sem, kept_sem, own_sem, gz_send, gz_recv, gx_send, gx_recv, gy_send, gy_recv, gp_send, gp_recv, c_send, c_recv, in_send, in_recv, x_send, x_recv, z_send, z_recv, o_send, o_recv,
 ):
     s = lax.axis_index("space")
     k = lax.axis_index("mode")
@@ -42,11 +42,18 @@
         dev(lax.rem(s + 16, NS), wrap(a + 2, NA) * NB + b),
     )
     x_up, x_down = dev(s, a * NB + wrap(b + 1, NB)), dev(s, a * NB + wrap(b - 1, NB))
+    z_pair = dev(lax.rem(s + 16, NS), k)
     y_up = dev(lo * 16 + wrap(y + 1, 8) * 2 + core, k)
     y_down = dev(lo * 16 + wrap(y - 1, 8) * 2 + core, k)
     partner = dev(s + 1 - 2 * core, k)
     right, left = dev(wrap(s + 1, NS), k), dev(wrap(s - 1, NS), k)
-    z_next, z_prev = dev(s, wrap(k + 1, NK)), dev(s, wrap(k - 1, NK))
+
+    def block_of(mode):
+        aa, bb = mode // NB, mode % NB
+        return aa * NB + bb + (aa % 2) * (NB - 1 - 2 * bb)
+
+    zb = block_of(k)
+    z_next, z_prev = dev(s, block_of(wrap(zb + 1, NK))), dev(s, block_of(wrap(zb - 1, NK)))
 
     def mode_peer(d):
         return wrap(k + d, NK)
@@ -67,16 +74,17 @@
     def _(d):
         pl.semaphore_signal(barrier, inc=1, device_id=dev(s, mode_peer(d)), device_id_type=MESH)
 
-    for peer in (right, left, z_peers[0], z_peers[2], y_up, y_down):
+    for peer in (right, left, z_peers[0], z_peers[2], z_pair, y_up, y_down):
         pl.semaphore_signal(barrier, inc=1, device_id=peer, device_id_type=MESH)
 
-    pl.semaphore_wait(barrier, NK - 1 + 6)
+    pl.semaphore_wait(barrier, NK - 1 + 7)
 
     own.wait()
     rows = [a, wrap(a + toward, NA), wrap(a - toward, NA), wrap(a + 2, NA)]
     cols = [b, wrap(b - 1, NB), wrap(b + 1, NB), wrap(b + 2, NB)]
-    mine_u = (y % 2) * 4 + core * 2
-    other_u = (1 - y % 2) * 4 + core * 2
+    parity = lax.rem(y + lo, 2)
+    mine_u = parity * 4 + core * 2
+    other_u = (1 - parity) * 4 + core * 2
     started = []
 
     def remote(block, send, recv, peer):
@@ -84,21 +92,25 @@
             src_ref=block, dst_ref=block, send_sem=send, recv_sem=recv, device_id=peer, device_id_type=MESH
         )
 
-    def z_copy(n, kind):
-        block = full.at[a, b, pl.ds(other_u if kind else mine_u, 2)]
-        return remote(block, gz_send.at[n, kind], gz_recv.at[n, kind], z_peers[n - 1])
-
-    def x_copy(n, step, kind=0):
+    def z_copy(n):
+        block = full.at[a, b, pl.ds(mine_u if n == 2 else other_u, 2)]
+        return remote(block, gz_send.at[n], gz_recv.at[n], z_peers[n - 1])
+
+    def x_copy(n, step):
         if step < 2:
-            block = full.at[rows[n], b, pl.ds(other_u if kind else mine_u, 2)]
+            block = full.at[rows[n], b, pl.ds(mine_u, 2)]
         else:
             block = full.at[rows[n], cols[step - 1], mine_u + step - 2]
-        return remote(block, gx_send.at[n, step, kind], gx_recv.at[n, step, kind], x_down if step % 2 else x_up)
+        return remote(block, gx_send.at[n, step], gx_recv.at[n, step], x_down if step % 2 else x_up)
 
     def y_copy(n, m, way):
         block = full.at[rows[n], cols[m], mine_u + way]
         return remote(block, gy_send.at[n, m, way], gy_recv.at[n, m, way], y_down if way else y_up)
 
+    def pair_copy(n, m):
+        there = (0, 2, 1, 3)[n]
+        return remote(full.at[rows[n], cols[m], pl.ds(mine_u, 2)], gp_send.at[n, m], gp_recv.at[there, m], z_pair)
+
     def core_copy(n, m, kind):
         block = full.at[rows[n], cols[m], pl.ds(other_u if kind else mine_u, 2)]
         return remote(block, c_send.at[n, m, kind], c_recv.at[n, m, kind], partner)
@@ -107,47 +119,43 @@
         copy.start()
         started.append(copy)
 
-    def whole(n, m):
-        return (n, m) in ((0, 0), (0, 1), (0, 2), (1, 0))
-
     def share(n, m):
-        if not whole(n, m):
+        if m == 1:
+            start(pair_copy(n, m))
+        else:
             start(y_copy(n, m, 0))
             start(y_copy(n, m, 1))
         start(core_copy(n, m, 0))
 
-    start(z_copy(1, 0))
+    start(z_copy(1))
     start(x_copy(0, 0))
     start(x_copy(0, 1))
-    start(z_copy(2, 0))
-    start(z_copy(3, 0))
-    start(x_copy(0, 0, 1))
-    start(x_copy(0, 1, 1))
-    start(z_copy(1, 1))
-
-    def a2a(src, dst, extra, extra_dst, send, recv, d):
-        there = mode_peer(d)
+    start(z_copy(2))
+    start(z_copy(3))
+
+    def a2a(pairs, send, recv, d):
         return [
             pltpu.make_async_remote_copy(
-                src_ref=s_.at[there], dst_ref=d_.at[k], send_sem=send.at[d, i], recv_sem=recv.at[d, i],
-                device_id=dev(s, there), device_id_type=MESH,
+                src_ref=src, dst_ref=dst, send_sem=send.at[d, i], recv_sem=recv.at[d, i],
+                device_id=dev(s, mode_peer(d)), device_id_type=MESH,
             )
-            for i, (s_, d_) in enumerate(((src, dst), (extra, extra_dst)))
+            for i, (src, dst) in enumerate(pairs)
         ]
 
     def a2a_in(d):
-        return a2a(q_sent, q_state, coef_sent, coefs, in_send, in_recv, d)
+        block = block_of(mode_peer(d))
+        pairs = (q_sent.at[block], q_state.at[k]), (coef_sent.at[block], coefs.at[k])
+        return a2a(pairs, in_send, in_recv, d)
 
     def a2a_out(d):
-        return a2a(q_final, q_landed, tail, tails, o_send, o_recv, d)
+        there = mode_peer(d)
+        pairs = (q_final.at[there], q_landed.at[zb]), (tail.at[there], tails.at[zb])
+        return a2a(pairs, o_send, o_recv, d)
 
     def quantized(values):
         most = jnp.max(jnp.abs(values), axis=0, keepdims=True)
         steps = jnp.where(most > 0.0, 32767.0 / most, 0.0)
         return jnp.round(values * steps).astype(jnp.int32).astype(jnp.int16), most * (1.0 / 32767.0)
-
-    def restored(q, step):
-        return q.astype(jnp.int32).astype(jnp.float32) * step
 
     for fetch in fetches:
         fetch.wait()
@@ -176,39 +184,46 @@
         for copy in a2a_in(d):
             copy.start()
 
-    q_state[k] = q_sent[k]
-    coefs[k] = coef_sent[k]
-
-    def gather_stage(n):
-        if 0 < n < 4:
-            z_copy(n, 0).wait_recv()
-            start(x_copy(n, 0))
-            start(x_copy(n, 1))
-            share(n, 0)
-        if 0 <= n - 1 < 4:
-            for m in (1, 2):
-                x_copy(n - 1, m - 1).wait_recv()
-                start(x_copy(n - 1, m + 1))
-            share(n - 1, 1)
-            share(n - 1, 2)
-        if 0 <= n - 2 < 4:
-            x_copy(n - 2, 2).wait_recv()
-            x_copy(n - 2, 3).wait_recv()
-            share(n - 2, 3)
-        if 0 <= n - 3 < 4:
-            for m in range(4):
-                if n - 3 or m:
-                    if not whole(n - 3, m):
-                        y_copy(n - 3, m, 0).wait_recv()
-                        y_copy(n - 3, m, 1).wait_recv()
-                    elif m:
-                        x_copy(0, m - 1, 1).wait_recv()
-                    else:
-                        z_copy(1, 1).wait_recv()
-                    start(core_copy(n - 3, m, 1))
-
-    for n in range(4):
-        gather_stage(n)
+    q_state[k] = q_sent[zb]
+    coefs[k] = coef_sent[zb]
+
+    def from_z(n):
+        z_copy(n).wait_recv()
+        start(x_copy(n, 0))
+        start(x_copy(n, 1))
+        share(n, 0)
+
+    def from_x(n):
+        for m in (1, 2):
+            x_copy(n, m - 1).wait_recv()
+            start(x_copy(n, m + 1))
+        share(n, 1)
+        share(n, 2)
+
+    def from_far_x(n):
+        x_copy(n, 2).wait_recv()
+        x_copy(n, 3).wait_recv()
+        share(n, 3)
+
+    def from_others(n):
+        for m in range(4):
+            if n or m:
+                if m == 1:
+                    pair_copy((0, 2, 1, 3)[n], m).wait_recv()
+                else:
+                    y_copy(n, m, 0).wait_recv()
+                    y_copy(n, m, 1).wait_recv()
+                start(core_copy(n, m, 1))
+
+    from_z(1)
+    from_x(0)
+    from_z(2)
+    from_far_x(0)
+    from_x(1)
+    from_z(3)
+    from_x(2)
+    from_far_x(1)
+    from_others(0)
 
     total = jnp.sum(warm_ref[...])
     zi = lax.broadcasted_iota(jnp.int32, (8, 8, MODES), 1)
@@ -263,7 +278,7 @@
     def advect(t, h, energy):
         for copy in halo_copies(t, h):
             copy.wait_recv()
-        return lax.fori_loop(h * H, h * H + H, functools.partial(advect_block, t), energy)
+        return lax.fori_loop(h * H, h * H + H, functools.partial(advect_block, t), energy, unroll=4)
 
     def offset(energy):
         thermal = jnp.sum(energy, axis=1, keepdims=True) / total
@@ -293,30 +308,36 @@
 
         send_halo(0, h)
 
-    gather_stage(4)
-    gather_stage(5)
+    from_x(3)
+    from_far_x(2)
+    from_others(1)
     thermal = offset(advect(0, 1, advect(0, 0, nothing)))
-    gather_stage(6)
-
-    for n in range(4):
+
+    def first_product(n):
         for m in range(4):
             if n or m:
                 core_copy(n, m, 0).wait_recv()
                 core_copy(n, m, 1).wait_recv()
-
-        @pl.loop(0, 2)
-        def _(pair):
-            r = rows[n]
-            w = full[r, pl.ds(pair * 2, 2)].reshape(2 * MODES, M)
-            product = lax.dot_general(lhs[...], w, nt, preferred_element_type=jnp.float32)
-            parts = lax.dot_general(wlhs[...], w, nt, preferred_element_type=jnp.float32)
-            both = parts[0:1] + parts[1:2] + parts[2:3]
-            for e in range(2):
-                j = r * NB + pair * 2 + e
-                rx = jnp.broadcast_to(both[:, e * MODES:(e + 1) * MODES], (8, MODES))
-                relax[j] = rx
-                state[j] = moved[j] - product[:, e * MODES:(e + 1) * MODES] + rx[0:1] * thermal
-                stage_halo(1, j)
+        r = rows[n]
+        w = full[r].reshape(4 * MODES, M)
+        product = lax.dot_general(lhs[...], w, nt, preferred_element_type=jnp.float32)
+        parts = lax.dot_general(wlhs[...], w, nt, preferred_element_type=jnp.float32)
+        both = parts[0:1] + parts[1:2] + parts[2:3]
+        for e in range(NB):
+            j = r * NB + e
+            rx = jnp.broadcast_to(both[:, e * MODES:(e + 1) * MODES], (8, MODES))
+            relax[j] = rx
+            state[j] = moved[j] - product[:, e * MODES:(e + 1) * MODES] + rx[0:1] * thermal
+            stage_halo(1, j)
+
+    from_far_x(3)
+    first_product(0)
+    from_others(2)
+    first_product(1)
+    first_product(2)
+    from_others(3)
+    first_product(3)
+
 
     for h in range(2):
         send_halo(1, h)
@@ -325,27 +346,28 @@
         last = t == ITERS - 1
         energy = advect(t, 0, nothing)
 
-        @pl.loop(0, H)
+        @pl.loop(0, NA)
         def _(n):
-            w = full[n // 2, pl.ds((n % 2) * 2, 2), :, :, 0:M // 2].reshape(2 * MODES, M // 2)
+            w = full[n, :, :, :, 0:M // 2].reshape(NB * MODES, M // 2)
             half[n] = lax.dot_general(lhs[:, 0:M // 2], w, nt, preferred_element_type=jnp.float32)
 
         thermal = offset(advect(t, 1, energy))
         if last:
-            lane = lax.broadcasted_iota(jnp.int32, (8, 8, MODES), 2)
-            mine = jnp.sum(jnp.where(lane == 8 * k + zi, thermal.reshape(8, 8, MODES), 0.0), axis=1)
-            tail[:, 0:8, :] = jnp.broadcast_to(mine[None], (NK, 8, MODES))
+            lane = lax.broadcasted_iota(jnp.int32, (64, MODES), 1)
+            cell = lax.broadcasted_iota(jnp.int32, (64, MODES), 0)
+            offsets = jnp.sum(jnp.where(lane == cell, thermal, 0.0), axis=0, keepdims=True)
+            offsets = jnp.broadcast_to(offsets, (8, MODES))
 
         def finish(n):
-            w = full[n // 2, pl.ds((n % 2) * 2, 2), :, :, M // 2:M].reshape(2 * MODES, M // 2)
+            w = full[n, :, :, :, M // 2:M].reshape(NB * MODES, M // 2)
             product = half[n] + lax.dot_general(lhs[:, M // 2:M], w, nt, preferred_element_type=jnp.float32)
-            for e in range(2):
-                j = 2 * n + e
+            for e in range(NB):
+                j = NB * n + e
                 new = moved[j] - product[:, e * MODES:(e + 1) * MODES] + relax[j, 0:1] * thermal
                 if last:
                     q, step = quantized(new)
                     q_final[j] = q
-                    tail[j, 8:16, :] = jnp.broadcast_to(step, (8, MODES))
+                    tail[j] = jnp.where(row == 1, jnp.broadcast_to(step, (8, MODES)), offsets)
                     d = lax.rem(j - k + NK, NK)
 
                     @pl.when(d > 0)
@@ -357,33 +379,30 @@
                     stage_halo(t + 1, j)
 
         if last:
-            @pl.loop(0, H)
+            @pl.loop(0, NA)
             def _(step):
-                finish(lax.rem(k // 2 + step, H))
+                finish(wrap(a + step, NA))
         else:
             for h in range(2):
-                @pl.loop(h * H // 2, (h + 1) * H // 2)
+                @pl.loop(h * NA // 2, (h + 1) * NA // 2)
                 def _(n):
                     finish(n)
 
                 send_halo(t + 1, h)
 
-    q_landed[k] = q_final[k]
-    tails[k] = tail[k]
+    kept = [
+        pltpu.make_async_copy(q_final.at[k], q_landed.at[zb], kept_sem.at[0]),
+        pltpu.make_async_copy(tail.at[k], tails.at[zb], kept_sem.at[1]),
+    ]
+    for copy in kept:
+        copy.start()
+    for copy in kept:
+        copy.wait()
 
     @pl.loop(1, NK)
     def _(d):
         for copy in a2a_out(d):
             copy.wait_recv()
-
-    @pl.loop(0, NK)
-    def _(j):
-        back[j] = restored(q_landed[j], tails[j, 8:9]).reshape(8, 8, MODES)
-
-    for xy in range(8):
-        cells = back[:, xy].reshape(MODES, MODES)
-        out_ref[pl.ds(xy, MODES, stride=8), :] = jnp.transpose(cells)
-    therm_ref[...] = jnp.sum(tails[:, 0:8, :], axis=0)
 
     @pl.loop(1, NK)
     def _(d):
@@ -398,18 +417,42 @@
                 copy.wait_send()
 
 
+def restored(q, step):
+    return q.astype(jnp.int32).astype(jnp.float32) * step
+
+
+def unpack(q_ref, tail_ref, out_ref, therm_ref, back):
+    @pl.loop(0, NK)
+    def _(j):
+        back[j] = restored(q_ref[j], tail_ref[j, 1:2]).reshape(8, 8, MODES)
+
+    for xy in range(8):
+        cells = back[:, xy].reshape(MODES, MODES)
+        out_ref[pl.ds(xy, MODES, stride=8), :] = jnp.transpose(cells)
+    lane = lax.broadcasted_iota(jnp.int32, (8, MODES), 1)
+    offsets = jnp.zeros((8, MODES), jnp.float32)
+    for j in range(NK):
+        cells = jnp.broadcast_to(tail_ref[j, 0:1], (8, MODES))
+        moved = pltpu.roll(cells, (8 * j - 56) % MODES, 1)
+        moved = pltpu.roll(moved, 0, 1, stride=8, stride_axis=0)
+        offsets = jnp.where(lane // 8 == j, moved, offsets)
+    for xy in range(8):
+        therm_ref[xy:xy + 1, :] = offsets[7 - xy:8 - xy]
+
+
 def shards(occupation, offset, warmth, courant, sign, matrix):
     f32, bf16 = jnp.float32, jnp.bfloat16
     dma = pltpu.SemaphoreType.DMA
     vmem = pl.BlockSpec(memory_space=pltpu.VMEM)
-    out, therm = pl.pallas_call(
+    hbm = pl.BlockSpec(memory_space=pltpu.HBM)
+    landed, tails = pl.pallas_call(
         kernel,
         out_shape=(
-            jax.ShapeDtypeStruct((8 * MODES, 128), f32),
-            jax.ShapeDtypeStruct((8, 128), f32),
+            jax.ShapeDtypeStruct((NK, 64, MODES), jnp.int16),
+            jax.ShapeDtypeStruct((NK, 8, MODES), f32),
         ),
-        in_specs=[pl.BlockSpec(memory_space=pltpu.HBM)] * 6,
-        out_specs=(vmem, vmem),
+        in_specs=[hbm] * 6,
+        out_specs=(hbm, hbm),
         scratch_shapes=[
             pltpu.VMEM((8 * MODES, 128), f32),
             pltpu.VMEM((8, 128), f32),
@@ -424,10 +467,7 @@
             pltpu.VMEM((NK, 8, MODES), f32),
             pltpu.VMEM((NK, 8, MODES), f32),
             pltpu.VMEM((NK, 64, MODES), jnp.int16),
-            pltpu.VMEM((NK, 64, MODES), jnp.int16),
-            pltpu.VMEM((NK, 16, MODES), f32),
-            pltpu.VMEM((NK, 16, MODES), f32),
-            pltpu.VMEM((NK, 8, 8, MODES), f32),
+            pltpu.VMEM((NK, 8, MODES), f32),
             pltpu.VMEM((64, M), bf16),
             pltpu.VMEM((16, M), bf16),
             pltpu.VMEM((NK, 8, MODES), f32),
@@ -436,12 +476,14 @@
             pltpu.VMEM((ITERS, 2, NK, 8, MODES), f32),
             pltpu.VMEM((ITERS, 2, NK, 8, MODES), f32),
             pltpu.VMEM((NK, 64, MODES), f32),
-            pltpu.VMEM((NK // 2, 64, 2 * MODES), f32),
+            pltpu.VMEM((NA, 64, NB * MODES), f32),
             dma((5,)),
+            dma((2,)),
             dma,
-            dma((4, 2)), dma((4, 2)),
+            dma((4,)), dma((4,)),
+            dma((4, 4)), dma((4, 4)),
             dma((4, 4, 2)), dma((4, 4, 2)),
-            dma((4, 4, 2)), dma((4, 4, 2)),
+            dma((4, 4)), dma((4, 4)),
             dma((4, 4, 2)), dma((4, 4, 2)),
             dma((NK, 2)), dma((NK, 2)),
             dma((ITERS, 2, 2)), dma((ITERS, 2, 2)),
@@ -460,6 +502,16 @@
         sign.reshape(1, MODES),
         matrix.reshape(8, 16, M),
     )
+    out, therm = pl.pallas_call(
+        unpack,
+        out_shape=(
+            jax.ShapeDtypeStruct((8 * MODES, 128), f32),
+            jax.ShapeDtypeStruct((8, 128), f32),
+        ),
+        in_specs=[vmem, vmem],
+        out_specs=(vmem, vmem),
+        scratch_shapes=[pltpu.VMEM((NK, 8, 8, MODES), f32)],
+    )(landed, tails)
     return out.reshape(occupation.shape), therm.reshape(offset.shape)
 
 

time: 92.1 us -> 85.7 us (0.931)
  Pallas kernels: 88.8 us -> 85 us
  local copies, waits for them, and re-layouts: 2.47 us -> 0 us
    pallas_call x1 -> x2, Pallas kernels: 88.8 us -> 85 us  [the longest x1 82.8 us: shards(): pl.pallas_call(kernel, out_shape=(jax.ShapeDtypeStruct((NK, 64, MODES), j...]
    unnamed x4 -> x0, local copies, waits for them, and re-layouts: 2.47 us -> none
where the time goes in v4:
time: 85.7 us; the launch traced here: 85.6 us
  Pallas kernels  85 us (99%)
    pallas_call x1, Pallas kernels, shards(): pl.pallas_call(kernel, out_shape=(jax.ShapeDtypeStruct((NK, 64, MODES), j...  82.8 us
    pallas_call x1, Pallas kernels, shards(): pl.pallas_call(unpack, out_shape=(jax.ShapeDtypeStruct((8 * MODES, 128),...  2.17 us

profile of v4, /device:TPU:6, one launch (start us, length us, event | category | flops | bytes accessed | tf_op | source)
XLA Modules:
  0.0 85.6 jit_solution(10445842570184419660)
XLA Ops:
  0.6 82.8 %shard_map.77 = (s16[16,64,128]{2,1,0:T(8,128)(2,1)}, f32[16,8,128]{2,1,0:T(8,128)}) custom-call(f32[1024,128]{1,0:T(8,128)} %bitcast.7, f32[8,128]{1,0:T(8,128)} %bitcast.11, f32[16,128]{1,0:T(8,128)} %bitcast.10, f32[3,128]{1,0:T(4,128)} %cour_hbm.1, s32[1,128]{1,0:T(1,128)} %bitcast.13, bf16[8,16,2048]{2,1,0:T(8,128)(2,1)} %bitcast.8), custom_call_target="tpu_custom_call" | custom-call | flops 1700000000 | bytes 2000000 | tf_op jit(solution)/shard_map/pallas_call | solution.py:448
  83.4 2.2 %shard_map.78 = (f32[1024,128]{1,0:T(8,128)}, f32[8,128]{1,0:T(8,128)}) custom-call(s16[16,64,128]{2,1,0:T(8,128)(2,1)} %get-tuple-element.6.q_ref, f32[16,8,128]{2,1,0:T(8,128)} %get-tuple-element.7.tail_ref), custom_call_target="tpu_custom_call" | custom-call | tf_op jit(solution)/shard_map/pallas_call | solution.py:505

commit v5 on v4

--- a/solution.py
+++ b/solution.py
@@ -20,7 +20,7 @@
     q_landed, tails,
     occ_ref, t0_ref, warm_ref, cour_ref, sign_ref,
     full, sent, state, q_sent, q_state, coef_sent, coefs, q_final, tail, lhs, wlhs, relax, xs, xr, zs, zr, moved, half,
-    fetch_sem, kept_sem, own_sem, gz_send, gz_recv, gx_send, gx_recv, gy_send, gy_recv, gp_send, gp_recv, c_send, c_recv, in_send, in_recv, x_send, x_recv, z_send, z_recv, o_send, o_recv,
+    fetch_sem, kept_sem, own_sem, gz_send, gz_recv, gx_send, gx_recv, gf_send, gf_recv, gy_send, gy_recv, gp_send, gp_recv, c_send, c_recv, in_send, in_recv, x_send, x_recv, z_send, z_recv, o_send, o_recv,
 ):
     s = lax.axis_index("space")
     k = lax.axis_index("mode")
@@ -36,11 +36,9 @@
 
     y = (s // 2) % 8
     toward = 2 * lo - 1
-    z_peers = (
-        dev(lax.rem(s + 16, NS), wrap(a + toward, NA) * NB + b),
-        dev(s, wrap(a + toward, NA) * NB + b),
-        dev(lax.rem(s + 16, NS), wrap(a + 2, NA) * NB + b),
-    )
+    z_near = dev(lax.rem(s + 16, NS), wrap(a + toward, NA) * NB + b)
+    z_over = dev(s, wrap(a + toward, NA) * NB + b)
+    z_back = dev(s, wrap(a - toward, NA) * NB + b)
     x_up, x_down = dev(s, a * NB + wrap(b + 1, NB)), dev(s, a * NB + wrap(b - 1, NB))
     z_pair = dev(lax.rem(s + 16, NS), k)
     y_up = dev(lo * 16 + wrap(y + 1, 8) * 2 + core, k)
@@ -70,14 +68,14 @@
     own.start()
     barrier = pltpu.get_barrier_semaphore()
 
+    for peer in (right, left, z_near, z_pair, y_up, y_down):
+        pl.semaphore_signal(barrier, inc=1, device_id=peer, device_id_type=MESH)
+
     @pl.loop(1, NK)
     def _(d):
         pl.semaphore_signal(barrier, inc=1, device_id=dev(s, mode_peer(d)), device_id_type=MESH)
 
-    for peer in (right, left, z_peers[0], z_peers[2], z_pair, y_up, y_down):
-        pl.semaphore_signal(barrier, inc=1, device_id=peer, device_id_type=MESH)
-
-    pl.semaphore_wait(barrier, NK - 1 + 7)
+    pl.semaphore_wait(barrier, NK - 1 + 6)
 
     own.wait()
     rows = [a, wrap(a + toward, NA), wrap(a - toward, NA), wrap(a + 2, NA)]
@@ -93,15 +91,16 @@
         )
 
     def z_copy(n):
-        block = full.at[a, b, pl.ds(mine_u if n == 2 else other_u, 2)]
-        return remote(block, gz_send.at[n], gz_recv.at[n], z_peers[n - 1])
-
-    def x_copy(n, step):
-        if step < 2:
-            block = full.at[rows[n], b, pl.ds(mine_u, 2)]
-        else:
-            block = full.at[rows[n], cols[step - 1], mine_u + step - 2]
-        return remote(block, gx_send.at[n, step], gx_recv.at[n, step], x_down if step % 2 else x_up)
+        block = full.at[rows[1] if n == 3 else a, b, pl.ds(other_u if n == 1 else mine_u, 2)]
+        return remote(block, gz_send.at[n], gz_recv.at[n], (z_near, z_over, z_back)[n - 1])
+
+    def x_copy(n, way):
+        block = full.at[rows[n], b, pl.ds(mine_u, 2)]
+        return remote(block, gx_send.at[n, way], gx_recv.at[n, way], x_down if way else x_up)
+
+    def far_copy(n, way):
+        block = full.at[rows[n], cols[1 + way], mine_u + way]
+        return remote(block, gf_send.at[n, way], gf_recv.at[n, way], x_down if way else x_up)
 
     def y_copy(n, m, way):
         block = full.at[rows[n], cols[m], mine_u + way]
@@ -131,7 +130,7 @@
     start(x_copy(0, 0))
     start(x_copy(0, 1))
     start(z_copy(2))
-    start(z_copy(3))
+
 
     def a2a(pairs, send, recv, d):
         return [
@@ -189,20 +188,22 @@
 
     def from_z(n):
         z_copy(n).wait_recv()
+        if n == 1:
+            start(z_copy(3))
         start(x_copy(n, 0))
         start(x_copy(n, 1))
         share(n, 0)
 
     def from_x(n):
-        for m in (1, 2):
-            x_copy(n, m - 1).wait_recv()
-            start(x_copy(n, m + 1))
+        for way in range(2):
+            x_copy(n, way).wait_recv()
+            start(far_copy(n, way))
         share(n, 1)
         share(n, 2)
 
     def from_far_x(n):
-        x_copy(n, 2).wait_recv()
-        x_copy(n, 3).wait_recv()
+        far_copy(n, 0).wait_recv()
+        far_copy(n, 1).wait_recv()
         share(n, 3)
 
     def from_others(n):
@@ -228,10 +229,9 @@
     total = jnp.sum(warm_ref[...])
     zi = lax.broadcasted_iota(jnp.int32, (8, 8, MODES), 1)
     nt = (((1,), (1,)), ((), ()))
-    H = NK // 2
 
     def halo_copies(t, h):
-        part = pl.ds(h * H, H)
+        part = pl.ds(h * NB, NB)
         return [
             pltpu.make_async_remote_copy(
                 src_ref=src.at[t, way, part], dst_ref=dst.at[t, way, part],
@@ -276,9 +276,11 @@
         return energy + mv_bf.astype(jnp.float32) * warm_ref[pl.ds(j, 1), :]
 
     def advect(t, h, energy):
-        for copy in halo_copies(t, h):
-            copy.wait_recv()
-        return lax.fori_loop(h * H, h * H + H, functools.partial(advect_block, t), energy, unroll=4)
+        for q in range(2 * h, 2 * h + 2):
+            for copy in halo_copies(t, q):
+                copy.wait_recv()
+            energy = lax.fori_loop(q * NB, q * NB + NB, functools.partial(advect_block, t), energy, unroll=4)
+        return energy
 
     def offset(energy):
         thermal = jnp.sum(energy, axis=1, keepdims=True) / total
@@ -300,17 +302,20 @@
         for copy in a2a_in(d):
             copy.wait_recv()
 
-    for h in range(2):
-        @pl.loop(h * H, h * H + H)
-        def _(j):
+    @pl.loop(0, NA)
+    def _(q):
+        @pl.loop(0, NB)
+        def _(e):
+            j = q * NB + e
             state[j] = restored(q_state[j], coefs[j, 6:7])
             stage_halo(0, j)
 
-        send_halo(0, h)
+        send_halo(0, q)
 
     from_x(3)
     from_far_x(2)
     from_others(1)
+    from_far_x(3)
     thermal = offset(advect(0, 1, advect(0, 0, nothing)))
 
     def first_product(n):
@@ -329,8 +334,8 @@
             relax[j] = rx
             state[j] = moved[j] - product[:, e * MODES:(e + 1) * MODES] + rx[0:1] * thermal
             stage_halo(1, j)
-
-    from_far_x(3)
+        send_halo(1, r)
+
     first_product(0)
     from_others(2)
     first_product(1)
@@ -339,16 +344,18 @@
     first_product(3)
 
 
-    for h in range(2):
-        send_halo(1, h)
-
     for t in range(1, ITERS):
         last = t == ITERS - 1
         energy = advect(t, 0, nothing)
+        order = [cols[3], cols[2], cols[1], b] if last else list(range(NB))
+
+        def weights(n, h):
+            part = slice(h * (M // 2), (h + 1) * (M // 2))
+            return jnp.concatenate([full[n, c, :, :, part].reshape(MODES, M // 2) for c in order], axis=0)
 
         @pl.loop(0, NA)
         def _(n):
-            w = full[n, :, :, :, 0:M // 2].reshape(NB * MODES, M // 2)
+            w = weights(n, 0)
             half[n] = lax.dot_general(lhs[:, 0:M // 2], w, nt, preferred_element_type=jnp.float32)
 
         thermal = offset(advect(t, 1, energy))
@@ -356,18 +363,17 @@
             lane = lax.broadcasted_iota(jnp.int32, (64, MODES), 1)
             cell = lax.broadcasted_iota(jnp.int32, (64, MODES), 0)
             offsets = jnp.sum(jnp.where(lane == cell, thermal, 0.0), axis=0, keepdims=True)
-            offsets = jnp.broadcast_to(offsets, (8, MODES))
 
         def finish(n):
-            w = full[n, :, :, :, M // 2:M].reshape(NB * MODES, M // 2)
+            w = weights(n, 1)
             product = half[n] + lax.dot_general(lhs[:, M // 2:M], w, nt, preferred_element_type=jnp.float32)
             for e in range(NB):
-                j = NB * n + e
+                j = NB * n + order[e]
                 new = moved[j] - product[:, e * MODES:(e + 1) * MODES] + relax[j, 0:1] * thermal
                 if last:
                     q, step = quantized(new)
                     q_final[j] = q
-                    tail[j] = jnp.where(row == 1, jnp.broadcast_to(step, (8, MODES)), offsets)
+                    tail[j] = jnp.concatenate([offsets, step], axis=0)
                     d = lax.rem(j - k + NK, NK)
 
                     @pl.when(d > 0)
@@ -381,14 +387,12 @@
         if last:
             @pl.loop(0, NA)
             def _(step):
-                finish(wrap(a + step, NA))
+                finish(wrap(a + 2 + step - 3 * (step // 2) - 2 * (step // 3), NA))
         else:
-            for h in range(2):
-                @pl.loop(h * NA // 2, (h + 1) * NA // 2)
-                def _(n):
-                    finish(n)
-
-                send_halo(t + 1, h)
+            @pl.loop(0, NA)
+            def _(n):
+                finish(n)
+                send_halo(t + 1, n)
 
     kept = [
         pltpu.make_async_copy(q_final.at[k], q_landed.at[zb], kept_sem.at[0]),
@@ -412,7 +416,7 @@
     for copy in started:
         copy.wait_send()
     for t in range(ITERS):
-        for h in range(2):
+        for h in range(NA):
             for copy in halo_copies(t, h):
                 copy.wait_send()
 
@@ -449,7 +453,7 @@
         kernel,
         out_shape=(
             jax.ShapeDtypeStruct((NK, 64, MODES), jnp.int16),
-            jax.ShapeDtypeStruct((NK, 8, MODES), f32),
+            jax.ShapeDtypeStruct((NK, 2, MODES), f32),
         ),
         in_specs=[hbm] * 6,
         out_specs=(hbm, hbm),
@@ -467,7 +471,7 @@
             pltpu.VMEM((NK, 8, MODES), f32),
             pltpu.VMEM((NK, 8, MODES), f32),
             pltpu.VMEM((NK, 64, MODES), jnp.int16),
-            pltpu.VMEM((NK, 8, MODES), f32),
+            pltpu.VMEM((NK, 2, MODES), f32),
             pltpu.VMEM((64, M), bf16),
             pltpu.VMEM((16, M), bf16),
             pltpu.VMEM((NK, 8, MODES), f32),
@@ -481,13 +485,14 @@
             dma((2,)),
             dma,
             dma((4,)), dma((4,)),
-            dma((4, 4)), dma((4, 4)),
+            dma((4, 2)), dma((4, 2)),
+            dma((4, 2)), dma((4, 2)),
             dma((4, 4, 2)), dma((4, 4, 2)),
             dma((4, 4)), dma((4, 4)),
             dma((4, 4, 2)), dma((4, 4, 2)),
             dma((NK, 2)), dma((NK, 2)),
-            dma((ITERS, 2, 2)), dma((ITERS, 2, 2)),
-            dma((ITERS, 2, 2)), dma((ITERS, 2, 2)),
+            dma((ITERS, 2, NA)), dma((ITERS, 2, NA)),
+            dma((ITERS, 2, NA)), dma((ITERS, 2, NA)),
             dma((NK, 2)), dma((NK, 2)),
         ],
         compiler_params=pltpu.CompilerParams(

time: 85.7 us -> 81.6 us (0.952)
  Pallas kernels: 85 us -> 80.1 us
    pallas_call x1, Pallas kernels: 82.8 us -> 77.9 us  [shards(): pl.pallas_call(kernel, out_shape=(jax.ShapeDtypeStruct((NK, 64, MODES), j...]
where the time goes in v5:
time: 81.6 us; the launch traced here: 80.8 us
  Pallas kernels  80.1 us (98%)
    pallas_call x1, Pallas kernels, shards(): pl.pallas_call(kernel, out_shape=(jax.ShapeDtypeStruct((NK, 64, MODES), j...  77.9 us
    pallas_call x1, Pallas kernels, shards(): pl.pallas_call(unpack, out_shape=(jax.ShapeDtypeStruct((8 * MODES, 128),...  2.17 us

profile of v5, /device:TPU:6, one launch (start us, length us, event | category | flops | bytes accessed | tf_op | source)
XLA Modules:
  0.0 80.8 jit_solution(13804276406758593462)
XLA Ops:
  0.6 77.9 %shard_map.77 = (s16[16,64,128]{2,1,0:T(8,128)(2,1)}, f32[16,2,128]{2,1,0:T(2,128)}) custom-call(f32[1024,128]{1,0:T(8,128)} %bitcast.7, f32[8,128]{1,0:T(8,128)} %bitcast.11, f32[16,128]{1,0:T(8,128)} %bitcast.10, f32[3,128]{1,0:T(4,128)} %cour_hbm.1, s32[1,128]{1,0:T(1,128)} %bitcast.13, bf16[8,16,2048]{2,1,0:T(8,128)(2,1)} %bitcast.8), custom_call_target="tpu_custom_call" | custom-call | flops 1700000000 | bytes 2000000 | tf_op jit(solution)/shard_map/pallas_call | solution.py:452
  78.6 2.2 %shard_map.78 = (f32[1024,128]{1,0:T(8,128)}, f32[8,128]{1,0:T(8,128)}) custom-call(s16[16,64,128]{2,1,0:T(8,128)(2,1)} %get-tuple-element.6.q_ref, f32[16,2,128]{2,1,0:T(2,128)} %get-tuple-element.7.tail_ref), custom_call_target="tpu_custom_call" | custom-call | tf_op jit(solution)/shard_map/pallas_call | solution.py:510

commit v6 on v5

--- a/solution.py
+++ b/solution.py
@@ -71,7 +71,7 @@
     for peer in (right, left, z_near, z_pair, y_up, y_down):
         pl.semaphore_signal(barrier, inc=1, device_id=peer, device_id_type=MESH)
 
-    @pl.loop(1, NK)
+    @pl.loop(1, NK, unroll=3)
     def _(d):
         pl.semaphore_signal(barrier, inc=1, device_id=dev(s, mode_peer(d)), device_id_type=MESH)
 
@@ -178,11 +178,6 @@
         q_sent[j] = q
         coef_sent[j] = jnp.where(row == 6, jnp.broadcast_to(step, (8, MODES)), coef)
 
-    @pl.loop(1, NK)
-    def _(d):
-        for copy in a2a_in(d):
-            copy.start()
-
     q_state[k] = q_sent[zb]
     coefs[k] = coef_sent[zb]
 
@@ -218,6 +213,12 @@
 
     from_z(1)
     from_x(0)
+
+    @pl.loop(1, NK, unroll=3)
+    def _(d):
+        for copy in a2a_in(lax.rem(d + 6, NK - 1) + 1):
+            copy.start()
+
     from_z(2)
     from_far_x(0)
     from_x(1)
@@ -297,7 +298,7 @@
         parts = jnp.where(row16 == 0, hi, jnp.where(row16 == 1, mid, jnp.where(row16 == 2, low, 0.0)))
         wlhs[:, j * MODES:(j + 1) * MODES] = parts.astype(jnp.bfloat16)
 
-    @pl.loop(1, NK)
+    @pl.loop(1, NK, unroll=3)
     def _(d):
         for copy in a2a_in(d):
             copy.wait_recv()
@@ -344,8 +345,25 @@
     first_product(3)
 
 
+    def halos_left(t):
+        for q in range(NA):
+            for copy in halo_copies(t, q):
+                copy.wait_send()
+
+    for copy in started:
+        copy.wait_send()
+
+    @pl.loop(1, NK, unroll=3)
+    def _(d):
+        for copy in a2a_in(d):
+            copy.wait_send()
+
+    halos_left(0)
+
     for t in range(1, ITERS):
         last = t == ITERS - 1
+        if t > 1:
+            halos_left(t - 1)
         energy = advect(t, 0, nothing)
         order = [cols[3], cols[2], cols[1], b] if last else list(range(NB))
 
@@ -353,7 +371,7 @@
             part = slice(h * (M // 2), (h + 1) * (M // 2))
             return jnp.concatenate([full[n, c, :, :, part].reshape(MODES, M // 2) for c in order], axis=0)
 
-        @pl.loop(0, NA)
+        @pl.loop(0, NA, unroll=2)
         def _(n):
             w = weights(n, 0)
             half[n] = lax.dot_general(lhs[:, 0:M // 2], w, nt, preferred_element_type=jnp.float32)
@@ -364,7 +382,7 @@
             cell = lax.broadcasted_iota(jnp.int32, (64, MODES), 0)
             offsets = jnp.sum(jnp.where(lane == cell, thermal, 0.0), axis=0, keepdims=True)
 
-        def finish(n):
+        def finish(n, own_row=False):
             w = weights(n, 1)
             product = half[n] + lax.dot_general(lhs[:, M // 2:M], w, nt, preferred_element_type=jnp.float32)
             for e in range(NB):
@@ -374,22 +392,18 @@
                     q, step = quantized(new)
                     q_final[j] = q
                     tail[j] = jnp.concatenate([offsets, step], axis=0)
-                    d = lax.rem(j - k + NK, NK)
-
-                    @pl.when(d > 0)
-                    def _():
-                        for copy in a2a_out(d):
+                    if not (own_row and e == NB - 1):
+                        for copy in a2a_out(lax.rem(j - k + NK, NK)):
                             copy.start()
                 else:
                     state[j] = new
                     stage_halo(t + 1, j)
 
         if last:
-            @pl.loop(0, NA)
-            def _(step):
-                finish(wrap(a + 2 + step - 3 * (step // 2) - 2 * (step // 3), NA))
+            for step in (2, 1, 3, 0):
+                finish(wrap(a + step, NA), step == 0)
         else:
-            @pl.loop(0, NA)
+            @pl.loop(0, NA, unroll=2)
             def _(n):
                 finish(n)
                 send_halo(t + 1, n)
@@ -400,25 +414,19 @@
     ]
     for copy in kept:
         copy.start()
+    halos_left(ITERS - 1)
     for copy in kept:
         copy.wait()
 
-    @pl.loop(1, NK)
+    @pl.loop(1, NK, unroll=3)
     def _(d):
         for copy in a2a_out(d):
             copy.wait_recv()
 
-    @pl.loop(1, NK)
+    @pl.loop(1, NK, unroll=3)
     def _(d):
-        for copy in a2a_in(d) + a2a_out(d):
+        for copy in a2a_out(d):
             copy.wait_send()
-
-    for copy in started:
-        copy.wait_send()
-    for t in range(ITERS):
-        for h in range(NA):
-            for copy in halo_copies(t, h):
-                copy.wait_send()
 
 
 def restored(q, step):

time: 81.6 us -> 80.6 us (0.988)
  no operation moved by 1% of the time
where the time goes in v6:
time: 80.6 us; the launch traced here: 80.4 us
  Pallas kernels  79.8 us (99%)
    pallas_call x1, Pallas kernels, shards(): pl.pallas_call(kernel, out_shape=(jax.ShapeDtypeStruct((NK, 64, MODES), j...  77.6 us
    pallas_call x1, Pallas kernels, shards(): pl.pallas_call(unpack, out_shape=(jax.ShapeDtypeStruct((8 * MODES, 128),...  2.17 us

profile of v6, /device:TPU:6, one launch (start us, length us, event | category | flops | bytes accessed | tf_op | source)
XLA Modules:
  0.0 80.4 jit_solution(4915504653052918628)
XLA Ops:
  0.6 77.6 %shard_map.77 = (s16[16,64,128]{2,1,0:T(8,128)(2,1)}, f32[16,2,128]{2,1,0:T(2,128)}) custom-call(f32[1024,128]{1,0:T(8,128)} %bitcast.7, f32[8,128]{1,0:T(8,128)} %bitcast.11, f32[16,128]{1,0:T(8,128)} %bitcast.10, f32[3,128]{1,0:T(4,128)} %cour_hbm.1, s32[1,128]{1,0:T(1,128)} %bitcast.13, bf16[8,16,2048]{2,1,0:T(8,128)(2,1)} %bitcast.8), custom_call_target="tpu_custom_call" | custom-call | flops 1700000000 | bytes 2000000 | tf_op jit(solution)/shard_map/pallas_call | solution.py:460
  78.3 2.2 %shard_map.78 = (f32[1024,128]{1,0:T(8,128)}, f32[8,128]{1,0:T(8,128)}) custom-call(s16[16,64,128]{2,1,0:T(8,128)(2,1)} %get-tuple-element.6.q_ref, f32[16,2,128]{2,1,0:T(2,128)} %get-tuple-element.7.tail_ref), custom_call_target="tpu_custom_call" | custom-call | tf_op jit(solution)/shard_map/pallas_call | solution.py:518

commit v7 on v6

--- a/solution.py
+++ b/solution.py
@@ -172,7 +172,7 @@
         coef = jnp.where(row == 2 * d, jnp.where(bit == 0, c, 0.0), coef)
         coef = jnp.where(row == 2 * d + 1, jnp.where(bit == 1, c, 0.0), coef)
 
-    @pl.loop(0, NK)
+    @pl.loop(0, NK, unroll=4)
     def _(j):
         q, step = quantized(sent[j])
         q_sent[j] = q
@@ -305,7 +305,7 @@
 
     @pl.loop(0, NA)
     def _(q):
-        @pl.loop(0, NB)
+        @pl.loop(0, NB, unroll=4)
         def _(e):
             j = q * NB + e
             state[j] = restored(q_state[j], coefs[j, 6:7])
@@ -434,7 +434,7 @@
 
 
 def unpack(q_ref, tail_ref, out_ref, therm_ref, back):
-    @pl.loop(0, NK)
+    @pl.loop(0, NK, unroll=8)
     def _(j):
         back[j] = restored(q_ref[j], tail_ref[j, 1:2]).reshape(8, 8, MODES)
 

time: 80.6 us -> 80.5 us (level)
  no operation moved by 1% of the time
where the time goes in v7:
time: 80.5 us; the launch traced here: 80.4 us
  Pallas kernels  79.7 us (99%)
    pallas_call x1, Pallas kernels, shards(): pl.pallas_call(kernel, out_shape=(jax.ShapeDtypeStruct((NK, 64, MODES), j...  77.6 us
    pallas_call x1, Pallas kernels, shards(): pl.pallas_call(unpack, out_shape=(jax.ShapeDtypeStruct((8 * MODES, 128),...  2.12 us

profile of v7, /device:TPU:6, one launch (start us, length us, event | category | flops | bytes accessed | tf_op | source)
XLA Modules:
  0.0 80.4 jit_solution(12637799885568003703)
XLA Ops:
  0.6 77.6 %shard_map.77 = (s16[16,64,128]{2,1,0:T(8,128)(2,1)}, f32[16,2,128]{2,1,0:T(2,128)}) custom-call(f32[1024,128]{1,0:T(8,128)} %bitcast.7, f32[8,128]{1,0:T(8,128)} %bitcast.11, f32[16,128]{1,0:T(8,128)} %bitcast.10, f32[3,128]{1,0:T(4,128)} %cour_hbm.1, s32[1,128]{1,0:T(1,128)} %bitcast.13, bf16[8,16,2048]{2,1,0:T(8,128)(2,1)} %bitcast.8), custom_call_target="tpu_custom_call" | custom-call | flops 1700000000 | bytes 2000000 | tf_op jit(solution)/shard_map/pallas_call | solution.py:460
  78.2 2.1 %shard_map.78 = (f32[1024,128]{1,0:T(8,128)}, f32[8,128]{1,0:T(8,128)}) custom-call(s16[16,64,128]{2,1,0:T(8,128)(2,1)} %get-tuple-element.6.q_ref, f32[16,2,128]{2,1,0:T(2,128)} %get-tuple-element.7.tail_ref), custom_call_target="tpu_custom_call" | custom-call | tf_op jit(solution)/shard_map/pallas_call | solution.py:518
